TPU v7x, 32 devices: a whole 2x2x4 slice. The times are simulated.
32 devices in a mesh: seq: 8 (over z, x), batch: 4 (over y, core).
Axes of the slice: x: 2, y: 2, z: 4, core: 2. Of those that a mesh axis runs over, the one named last changes fastest.
Arguments:
- hidden_in: bfloat16 [4, 2048, 1024], P('batch', 'seq'), may hold values from -6 to 6
- out_grad: bfloat16 [4, 2048, 1024], P('batch', 'seq'), may hold values from -6 to 6
- norm_gain_pair: float32 [2, 1024], replicated, may hold values from 0.5 to 1.5
- norm_bias_pair: float32 [2, 1024], replicated, may hold values from -1.2 to 1.2
- w_qkv: bfloat16 [1024, 3072], replicated, may hold values from -0.1875 to 0.1875
- qv_bias: float32 [2, 1024], replicated, may hold values from -1.2 to 1.2
- w_out: bfloat16 [1024, 1024], replicated, may hold values from -1.5 to 1.5
- out_bias: float32 [1024], replicated, may hold values from -1.2 to 1.2
- w_in_exp: bfloat16 [16, 1024, 4096], P('seq', None, 'batch'), may hold values from -0.1875 to 0.1875
- b_in_exp: float32 [16, 4096], P('seq', 'batch'), may hold values from -0.9 to 0.9
- w_out_exp: bfloat16 [16, 4096, 1024], P('seq', 'batch'), may hold values from -0.125 to 0.125
- b_out_exp: float32 [16, 1024], P('seq'), may hold values from -0.6 to 0.6
- expert_ids: int32 [4, 2048, 1], P('batch', 'seq'), may hold values from 0 to 15; in each aligned block of 256 rows (0 to 255, 256 to 511, ..., all dimensions but the last counted through in order) at most 24 rows name the same one
- doc_lengths: int32 [4, 8], P('batch'), may hold values from 1 to 1794, 2048 in all within a row
- pad_mask: int32 [4, 2048], P('batch', 'seq'), may hold values 0 or 1
Outputs:
- output: bfloat16 [4, 2048, 1024], P('batch', 'seq')
- input_grad: bfloat16 [4, 2048, 1024], P('batch', 'seq')
- grad_norm_gains: float32 [2, 1024], P(None, ('seq', 'batch'))
- grad_norm_biases: float32 [2, 1024], P(None, ('seq', 'batch'))
- grad_w_qkv: float32 [1024, 3072], P(('seq', 'batch'))
- grad_qv_bias: float32 [2, 1024], P(None, ('seq', 'batch'))
- grad_w_out: float32 [1024, 1024], P(('seq', 'batch'))
- grad_out_bias: float32 [1024], P(('seq', 'batch'))
- grad_w_in_exp: float32 [16, 1024, 4096], P('seq', None, 'batch')
- grad_b_in_exp: float32 [16, 4096], P('seq', 'batch')
- grad_w_out_exp: float32 [16, 4096, 1024], P('seq', 'batch')
- grad_b_out_exp: float32 [16, 1024], P('seq')
Inputs may be any that keep to these rules, and one draw needn't show every extreme that they name: `expert_ids`: among the 256 tokens of one device no expert is named more than 24 times, and in some devices one expert is named exactly 24 times. `doc_lengths`: each row's 8 lengths sum to 2048, and its longest dialogue has exactly 1794 positions.
All inputs are finite; a program needn't handle non-finite values. No bound on the sum of `pad_mask` on one device may be relied on, other than what follows from the above.
Results may differ from a plain program's by a relative error of at most 0.015.
Values may be sent and summed in bfloat16 or wider, within the bound.
No kernel may reach another device: no remote copies, remote signals or barrier semaphores. Data moves between devices by JAX's collectives and lax.ppermute only.
A program may use at most 256 MiB of HBM per device.

v0:
```python
import math

import jax
import jax.numpy as jnp
from jax import lax
from jax.sharding import PartitionSpec as P

D = 1024
HEADS = 16
HEAD_DIM = 64
EXP_DEV = 2


EPS = 1e-05
NEG = -1e30


def layer_normalize(values, gain, shift):
    centre = values - jnp.mean(values, axis=-1, keepdims=True)
    spread = jnp.mean(centre * centre, axis=-1, keepdims=True)
    inv_std = lax.rsqrt(spread + EPS)
    normed = centre * inv_std
    return (normed * gain + shift, normed, inv_std)


def norm_backward_pass(grads, normed, inv_std, gain):
    scaled = grads * gain
    first_mean = jnp.mean(scaled, axis=-1, keepdims=True)
    second_mean = jnp.mean(scaled * normed, axis=-1, keepdims=True)
    return (
        inv_std * (scaled - first_mean - normed * second_mean),
        jnp.sum(grads * normed, axis=0),
        jnp.sum(grads, axis=0),
    )


def doc_of(positions, doc_ends):
    return jnp.sum((positions[:, None] >= doc_ends[None, :]).astype(jnp.int32), axis=1)


def allowed_pairs(q_pos, q_doc, k_pos, k_doc, k_pad):
    same_doc = q_doc[:, None] == k_doc[None, :]
    before = k_pos[None, :] <= q_pos[:, None]
    usable = (k_pad[None, :] == 1) | (k_pos[None, :] == q_pos[:, None])
    return same_doc & before & usable


def over_blocks(step_fn, totals, arrays, first_row):
    row_count = arrays[0].shape[0]
    block_rows = math.gcd(row_count, 512)

    def advance(current, block_index):
        pieces = tuple(
            (
                lax.dynamic_slice_in_dim(member, block_index * block_rows, block_rows, 0)
                for member in arrays
            )
        )
        return (step_fn(current, pieces, first_row + block_index * block_rows), None)

    result, _ = lax.scan(advance, totals, jnp.arange(row_count // block_rows, dtype=jnp.int32))
    return result


def key_grads(
    query_h, dout_h, lse_rows, delta_rows, q_pos, q_doc, key_h, value_h, k_pos, k_doc, k_pad
):
    allowed = allowed_pairs(q_pos, q_doc, k_pos, k_doc, k_pad)
    scores = jnp.einsum("qhd,khd->hqk", query_h, key_h, preferred_element_type=jnp.float32)
    probs = jnp.where(allowed[None], jnp.exp(scores - lse_rows.T[:, :, None]), 0.0)
    dprobs = jnp.einsum("qhd,khd->hqk", dout_h, value_h, preferred_element_type=jnp.float32)
    dscores = (probs * (dprobs - delta_rows.T[:, :, None])).astype(jnp.bfloat16)
    grad_keys = jnp.einsum("hqk,qhd->khd", dscores, query_h, preferred_element_type=jnp.float32)
    grad_values = jnp.einsum(
        "hqk,qhd->khd", probs.astype(jnp.bfloat16), dout_h, preferred_element_type=jnp.float32
    )
    return (grad_keys, grad_values)


def gelu_exact(values):
    return jax.nn.gelu(values, approximate=False)


def local(
    hidden_in,
    out_grad,
    norm_gain_pair,
    norm_bias_pair,
    w_qkv,
    qv_bias,
    w_out,
    out_bias,
    w_in_exp,
    b_in_exp,
    w_out_exp,
    b_out_exp,
    expert_ids,
    doc_lengths,
    pad_mask,
):
    tok_rows = hidden_in.shape[1]
    seq_count = lax.axis_size("seq")
    experts_all = EXP_DEV * seq_count
    capacity = max(2, 3 * tok_rows // (2 * experts_all))
    scale = HEAD_DIM ** (-0.5)
    input_tokens = hidden_in[0].astype(jnp.float32)
    first_normalized, first_centred_scaled, first_inverse_deviation = layer_normalize(
        input_tokens, norm_gain_pair[0], norm_bias_pair[0]
    )
    h_one = first_normalized.astype(jnp.bfloat16)
    mixed = jnp.dot(h_one, w_qkv, preferred_element_type=jnp.float32)
    queries = ((mixed[:, :D] + qv_bias[0]) * scale).astype(jnp.bfloat16)
    keys_vals = jnp.concatenate(
        [mixed[:, D : 2 * D], mixed[:, 2 * D :] + qv_bias[1][None, :]], axis=1
    ).astype(jnp.bfloat16)
    query_h = queries.reshape(tok_rows, HEADS, HEAD_DIM)
    q_pos = lax.axis_index("seq") * tok_rows + jnp.arange(tok_rows, dtype=jnp.int32)
    doc_ends = jnp.cumsum(doc_lengths[0])
    q_doc = doc_of(q_pos, doc_ends)
    key_pad = pad_mask[0]

    def split_keys(pieces, first_row):
        block_kv, block_pad = pieces
        row_count = block_kv.shape[0]
        key_h = block_kv[:, :D].reshape(row_count, HEADS, HEAD_DIM)
        value_h = block_kv[:, D:].reshape(row_count, HEADS, HEAD_DIM)
        k_pos = first_row + jnp.arange(row_count, dtype=jnp.int32)
        allowed = allowed_pairs(q_pos, q_doc, k_pos, doc_of(k_pos, doc_ends), block_pad)
        scores = jnp.einsum("thd,khd->htk", query_h, key_h, preferred_element_type=jnp.float32)
        return (key_h, value_h, allowed, jnp.where(allowed[None], scores, NEG))

    def stats_step(current, pieces, first_row):
        _, _, allowed, scores = split_keys(pieces, first_row)
        top_now, mass_now = current
        new_top = jnp.maximum(top_now, jnp.max(scores, axis=-1))
        weights = jnp.where(allowed[None], jnp.exp(scores - new_top[:, :, None]), 0.0)
        return (new_top, mass_now * jnp.exp(top_now - new_top) + jnp.sum(weights, axis=-1))

    def output_step(current, pieces, first_row):
        _, value_h, allowed, scores = split_keys(pieces, first_row)
        probs = jnp.where(allowed[None], jnp.exp(scores - log_mass[:, :, None]), 0.0).astype(
            jnp.bfloat16
        )
        return current + jnp.einsum(
            "htk,khd->thd", probs, value_h, preferred_element_type=jnp.float32
        )

    def dquery_step(current, pieces, first_row):
        key_h, value_h, allowed, scores = split_keys(pieces, first_row)
        probs = jnp.where(allowed[None], jnp.exp(scores - log_mass[:, :, None]), 0.0)
        dprobs = jnp.einsum("thd,khd->htk", dout_h, value_h, preferred_element_type=jnp.float32)
        dscores = (probs * (dprobs - delta[:, :, None])).astype(jnp.bfloat16)
        return current + jnp.einsum(
            "htk,khd->thd", dscores, key_h, preferred_element_type=jnp.float32
        )

    head_zeros = jnp.zeros((tok_rows, HEADS, HEAD_DIM), jnp.float32)
    init_stats = (
        jnp.full((HEADS, tok_rows), NEG, jnp.float32),
        jnp.zeros((HEADS, tok_rows), jnp.float32),
    )
    all_kv, all_pad = (
        lax.all_gather(keys_vals, "seq", axis=0, tiled=True),
        lax.all_gather(key_pad, "seq", axis=0, tiled=True),
    )

    def run_keys(step_fn, totals):
        return over_blocks(step_fn, totals, (all_kv, all_pad), 0)

    top_all, mass_all = run_keys(stats_step, init_stats)
    log_mass = top_all + jnp.log(mass_all)
    attended = run_keys(output_step, head_zeros)
    attended_b = attended.reshape(tok_rows, D).astype(jnp.bfloat16)
    branch = jnp.dot(attended_b, w_out, preferred_element_type=jnp.float32) + out_bias
    first_residual_input = input_tokens + branch
    second_normalized, second_centred_scaled, second_inverse_deviation = layer_normalize(
        first_residual_input, norm_gain_pair[1], norm_bias_pair[1]
    )
    x_two = second_normalized.astype(jnp.bfloat16)
    token_ids = expert_ids[0, :, 0]
    onehot = (token_ids[:, None] == jnp.arange(experts_all, dtype=jnp.int32)[None, :]).astype(
        jnp.int32
    )
    ranks = jnp.sum((jnp.cumsum(onehot, axis=0) - onehot) * onehot, axis=1)
    target = token_ids * capacity + ranks
    dispatch = (
        jnp.arange(experts_all * capacity, dtype=jnp.int32)[:, None] == target[None, :]
    ).astype(jnp.bfloat16)
    sent_rows = (
        jnp.dot(dispatch, x_two, preferred_element_type=jnp.float32)
        .astype(jnp.bfloat16)
        .reshape(seq_count, EXP_DEV, capacity, D)
    )
    rows_all = lax.all_gather(
        lax.all_to_all(sent_rows, "seq", split_axis=0, concat_axis=0, tiled=True),
        "batch",
        axis=0,
        tiled=True,
    )
    pre_act = (
        jnp.einsum("recd,edf->recf", rows_all, w_in_exp, preferred_element_type=jnp.float32)
        + b_in_exp[None, :, None, :]
    )
    hidden = gelu_exact(pre_act).astype(jnp.bfloat16)
    part_sums = jnp.einsum("recf,efd->recd", hidden, w_out_exp, preferred_element_type=jnp.float32)
    summed = lax.psum_scatter(
        part_sums.astype(jnp.bfloat16), "batch", scatter_dimension=0, tiled=True
    ).astype(jnp.float32)
    produced = (summed + b_out_exp[None, :, None, :]).astype(jnp.bfloat16)
    returned = lax.all_to_all(produced, "seq", split_axis=0, concat_axis=0, tiled=True)
    expert_rows = jnp.einsum(
        "st,sd->td",
        dispatch,
        returned.reshape(experts_all * capacity, D),
        preferred_element_type=jnp.float32,
    )
    output = (first_residual_input + expert_rows).astype(jnp.bfloat16)
    dout = out_grad[0].astype(jnp.float32)
    sent_grads = (
        jnp.dot(dispatch, out_grad[0], preferred_element_type=jnp.float32)
        .astype(jnp.bfloat16)
        .reshape(seq_count, EXP_DEV, capacity, D)
    )
    arrived_rows, arrived_grads = (
        lax.all_to_all(sent_rows, "seq", split_axis=0, concat_axis=0, tiled=True),
        lax.all_to_all(sent_grads, "seq", split_axis=0, concat_axis=0, tiled=True),
    )
    rows_all, grads_all = (
        lax.all_gather(arrived_rows, "batch", axis=0, tiled=True),
        lax.all_gather(arrived_grads, "batch", axis=0, tiled=True),
    )
    pre_act = (
        jnp.einsum("recd,edf->recf", rows_all, w_in_exp, preferred_element_type=jnp.float32)
        + b_in_exp[None, :, None, :]
    )
    hidden_f, gelu_back = jax.vjp(gelu_exact, pre_act)
    hidden_b = hidden_f.astype(jnp.bfloat16)
    dhidden = jnp.einsum(
        "recd,efd->recf", grads_all, w_out_exp, preferred_element_type=jnp.float32
    ).astype(jnp.bfloat16)
    dpre = gelu_back(dhidden.astype(jnp.float32))[0].astype(jnp.bfloat16)
    grad_w_out_exp = jnp.einsum(
        "recf,recd->efd", hidden_b, grads_all, preferred_element_type=jnp.float32
    )
    grad_b_out_exp = jnp.sum(grads_all, axis=(0, 2), dtype=jnp.float32)
    grad_w_in_exp = jnp.einsum("recd,recf->edf", rows_all, dpre, preferred_element_type=jnp.float32)
    grad_b_in_exp = jnp.sum(dpre, axis=(0, 2), dtype=jnp.float32)
    drows = jnp.einsum("recf,edf->recd", dpre, w_in_exp, preferred_element_type=jnp.float32)
    drows_sum = lax.psum_scatter(
        drows.astype(jnp.bfloat16), "batch", scatter_dimension=0, tiled=True
    )
    drows_home = lax.all_to_all(drows_sum, "seq", split_axis=0, concat_axis=0, tiled=True)
    second_residual_gradient = jnp.einsum(
        "st,sd->td",
        dispatch,
        drows_home.reshape(experts_all * capacity, D),
        preferred_element_type=jnp.float32,
    )
    second_norm_gradient, second_gain_gradient, second_shift_gradient = norm_backward_pass(
        second_residual_gradient, second_centred_scaled, second_inverse_deviation, norm_gain_pair[1]
    )
    d_one = dout + second_norm_gradient
    d_one_b = d_one.astype(jnp.bfloat16)
    grad_w_out = jnp.einsum("td,te->de", attended_b, d_one_b, preferred_element_type=jnp.float32)
    grad_out_bias = jnp.sum(d_one, axis=0)
    dout_b = jnp.einsum("te,de->td", d_one_b, w_out, preferred_element_type=jnp.float32).astype(
        jnp.bfloat16
    )
    dout_h = dout_b.reshape(tok_rows, HEADS, HEAD_DIM)
    delta = jnp.einsum("thd,thd->ht", dout_h.astype(jnp.float32), attended)
    dquery = run_keys(dquery_step, head_zeros)
    lse_rows = log_mass.T
    delta_rows = delta.T
    block_rows = math.gcd(tok_rows * lax.axis_size("seq"), 512)

    def one_block(block_index):
        first_key = block_index * block_rows
        block_kv = lax.dynamic_slice_in_dim(all_kv, first_key, block_rows, 0)
        block_pad = lax.dynamic_slice_in_dim(all_pad, first_key, block_rows, 0)
        k_pos = first_key + jnp.arange(block_rows, dtype=jnp.int32)
        grad_k, grad_v = key_grads(
            query_h,
            dout_h,
            lse_rows,
            delta_rows,
            q_pos,
            q_doc,
            block_kv[:, :D].reshape(block_rows, HEADS, HEAD_DIM),
            block_kv[:, D:].reshape(block_rows, HEADS, HEAD_DIM),
            k_pos,
            doc_of(k_pos, doc_ends),
            block_pad,
        )
        return jnp.concatenate(
            [grad_k.reshape(block_rows, D), grad_v.reshape(block_rows, D)], axis=1
        )

    blocks = lax.map(
        one_block, jnp.arange(tok_rows * lax.axis_size("seq") // block_rows, dtype=jnp.int32)
    )
    key_terms = lax.psum_scatter(
        blocks.reshape(tok_rows * lax.axis_size("seq"), 2 * D).astype(jnp.bfloat16),
        "seq",
        scatter_dimension=0,
        tiled=True,
    )
    dq_b = dquery.reshape(tok_rows, D).astype(jnp.bfloat16)
    dmixed = jnp.concatenate([dq_b * scale, key_terms], axis=1)
    grad_w_qkv = jnp.einsum("td,te->de", h_one, dmixed, preferred_element_type=jnp.float32)
    first_hidden_gradient = jnp.einsum(
        "te,de->td", dmixed, w_qkv, preferred_element_type=jnp.float32
    )
    first_norm_gradient, first_gain_gradient, first_shift_gradient = norm_backward_pass(
        first_hidden_gradient, first_centred_scaled, first_inverse_deviation, norm_gain_pair[0]
    )
    input_grad = (d_one + first_norm_gradient).astype(jnp.bfloat16)
    grad_q_bias = jnp.sum(dmixed[:, :D], axis=0, dtype=jnp.float32)
    grad_v_bias = jnp.sum(key_terms[:, D:], axis=0, dtype=jnp.float32)
    small_grads = jnp.stack(
        [
            first_gain_gradient,
            second_gain_gradient,
            first_shift_gradient,
            second_shift_gradient,
            grad_q_bias,
            grad_v_bias,
            grad_out_bias,
        ]
    )
    shared_qkv, shared_out, shared_small = (
        lax.psum_scatter(grad_w_qkv, ("seq", "batch"), scatter_dimension=0, tiled=True),
        lax.psum_scatter(grad_w_out, ("seq", "batch"), scatter_dimension=0, tiled=True),
        lax.psum_scatter(small_grads, ("seq", "batch"), scatter_dimension=1, tiled=True),
    )
    return (
        output[None],
        input_grad[None],
        shared_small[0:2],
        shared_small[2:4],
        shared_qkv,
        shared_small[4:6],
        shared_out,
        shared_small[6],
        grad_w_in_exp,
        grad_b_in_exp,
        grad_w_out_exp,
        grad_b_out_exp,
    )


def solution(mesh):
    return jax.shard_map(
        local,
        mesh=mesh,
        in_specs=(
            P("batch", "seq", None),
            P("batch", "seq", None),
            P(),
            P(),
            P(),
            P(),
            P(),
            P(),
            P("seq", None, "batch"),
            P("seq", "batch"),
            P("seq", "batch", None),
            P("seq", None),
            P("batch", "seq", None),
            P("batch", None),
            P("batch", "seq"),
        ),
        out_specs=(
            P("batch", "seq", None),
            P("batch", "seq", None),
            P(None, ("seq", "batch")),
            P(None, ("seq", "batch")),
            P(("seq", "batch"), None),
            P(None, ("seq", "batch")),
            P(("seq", "batch"), None),
            P(("seq", "batch")),
            P("seq", None, "batch"),
            P("seq", "batch"),
            P("seq", "batch", None),
            P("seq", None),
        ),
        check_vma=False,
    )
```

profile of v0, /device:TPU:0, one launch (start us, length us, event | category | flops | bytes accessed | tf_op | source)
XLA Modules:
  0.0 1157.0 jit_solution(15275432724424604910)
XLA Ops:
  12.3 4.9 fusion.140
  20.0 22.4 %all-gather = s32[1,2048]{1,0:T(1,128)S(1)} all-gather(s32[1,256]{1,0:T(1,128)S(1)} %copy-done.28), channel_id=2, replica_groups=mesh['seq'=8,'batch'=4] {'seq'}, dimensions={1}, use_global_device_ids=true | all-gather | bytes 9216 | tf_op jit(solution)/shard_map/all_gather | solution.py:164
  42.5 103.9 %all-gather.5.cloned.1.call-done = bf16[2048,2048]{1,0:T(8,128)(2,1)} async-done(((bf16[256,2048]{1,0:T(8,128)(2,1)}), bf16[2048,2048]{1,0:T(8,128)(2,1)}) %all-gather.5.cloned.1.call-update) | async-done | bytes 8388624 | tf_op jit(solution)/shard_map/all_gather | solution.py:163
  146.4 12.2 %copy.105 = bf16[2048,2048]{0,1:T(8,128)(2,1)} copy(bf16[2048,2048]{1,0:T(8,128)(2,1)} %all-gather.5.cloned.1.call-done) | data formatting | bytes 16777216
  158.7 51.5 %while.47 = (s32[]{:T(128)}, f32[16,256]{1,0:T(8,128)S(1)}, f32[16,256]{1,0:T(8,128)S(1)}, s32[256]{0:T(256)S(1)}, s32[4]{0:T(128)S(1)}, /*index=5*/s32[8]{0:T(1...) while((s32[]{:T(128)}, f32[16,256]{1,0:T(8,128)S(1)}, ...), condition=%wide.region_8.9_spmd.clone, body=%wide.region_4.8_spmd.clone.sunk | while | flops 281838336 | bytes 21070080 | solution.py:61
  161.7 4.8 fusion.229
  166.4 5.1 select_reduce_fusion.2
  174.5 4.8 fusion.229
  179.3 5.1 select_reduce_fusion.2
  187.4 4.8 fusion.229
  192.2 5.1 select_reduce_fusion.2
  200.3 4.8 fusion.229
  205.1 5.1 select_reduce_fusion.2
  210.3 40.6 %while.48 = (s32[]{:T(128)}, f32[256,16,64]{0,2,1:T(8,128)}, s32[4]{0:T(128)S(1)}, bf16[2048,2048]{0,1:T(8,128)(2,1)}, s32[256]{0:T(256)S(1)}, /*index=5*/s32[8]...) while((s32[]{:T(128)}, f32[256,16,64]{0,2,1:T(8,128)}, ...), condition=%wide.region_11.12_spmd.clone, body=%wide.region_9.11_spmd.clone.sunk | while | flops 546583296 | bytes 9208089 | solution.py:61
  211.5 3.0 constant_dynamic-slice_fusion.7
  215.0 5.2 fusion.235
  221.4 3.0 constant_dynamic-slice_fusion.7
  224.9 5.5 fusion.235
  231.7 3.0 constant_dynamic-slice_fusion.7
  235.1 5.5 fusion.235
  241.9 3.0 constant_dynamic-slice_fusion.7
  245.4 5.5 fusion.235
  254.6 22.8 %all_to_all.21 = bf16[8,2,24,1024]{3,2,1,0:T(8,128)(2,1)S(1)} all-to-all(bf16[8,2,24,1024]{3,2,1,0:T(8,128)(2,1)S(1)} %bitcast.453), channel_id=1, replica_groups=mesh['seq'=8,'batch'=4] {'seq'}, dimensions={0} | all-to-all | bytes 1572864 | tf_op jit(solution)/shard_map/all_to_all | solution.py:195
  280.1 23.2 %all_to_all.22 = bf16[8,2,24,1024]{3,2,1,0:T(8,128)(2,1)S(1)} all-to-all(bf16[8,2,24,1024]{3,2,1,0:T(8,128)(2,1)S(1)} %bitcast.452), channel_id=1, replica_groups=mesh['seq'=8,'batch'=4] {'seq'}, dimensions={0} | all-to-all | bytes 1572864 | tf_op jit(solution)/shard_map/all_to_all | solution.py:226
  306.1 20.8 %fusion.67 = (bf16[32,2,24,1024]{3,2,0,1:T(8,128)(2,1)}, f32[32,2,24,1024]{3,2,0,1:T(8,128)}, f32[2,32,24,1024]{3,2,1,0:T(8,128)}) fusion(f32[2,1024]{1,0:T(2,128)S(1)} %copy-done.30, bf16[32,2,24,1024]{3,2,0,1:T(8,128)(2,1)} %all-gather.7.cloned.1.call-done, bf16[2,1024,1024]{2,1,0:T(8,128)(2,1)} %param.31), kind=kOutput, calls=%fused_computation.91 | convolution fusion | flops 3325034496 | bytes 23076864 | tf_op jit(solution)/shard_map/recd,edf->recf/dot_general | solution.py:201
  326.9 9.3 all-gather.9.cloned.1.call-done
  336.2 13.0 %convert_reduce_fusion.5 = (f32[2,1024]{1,0:T(2,128)}, bf16[32,2,24,1024]{3,2,0,1:T(8,128)(2,1)S(1)}) fusion(f32[32,2,24,1024]{3,2,0,1:T(8,128)} %get-tuple-element.708, bf16[32,2,24,1024]{3,2,0,1:T(8,128)(2,1)} %all-gather.9.cloned.1.call-done, bf16[2,1024,1024]{2,1,0:T(8,128)(2,1)} %param.33, f32[2,32,24,1024]{3,2,1,0:T(8,128)} %get-tuple-element.730, ...), kind=kOutput, calls=%fused_computation.93 | convolution fusion | flops 3251107840 | bytes 23085056 | tf_op jit(solution)/shard_map/recd,efd->recf/dot_general | solution.py:238
  349.2 4.1 convert_bitcast_fusion
  353.8 3.4 copy.165
  357.3 38.1 %reduce-scatter.23.cloned.1.call-done = bf16[8,49152]{1,0:T(8,128)(2,1)} async-done(((bf16[32,49152]{1,0:T(8,128)(2,1)}), bf16[8,49152]{1,0:T(8,128)(2,1)}) %reduce-scatter.23.cloned.1.call-update) | async-done | bytes 786448
  397.8 5.5 all-to-all-start.3
  403.4 20.2 %all-to-all-done.3 = bf16[8,2,24,1024]{3,2,1,0:T(8,128)(2,1)} async-done(((bf16[8,2,24,1024]{3,2,1,0:T(8,128)(2,1)}), bf16[8,2,24,1024]{3,2,1,0:T(8,128)(2,1)}, u32[]{:S(2)}, u32[]{:S(2)}) %all-to-all-start.3) | async-done | bytes 786464 | tf_op jit(solution)/shard_map/all_to_all | solution.py:252
  432.8 95.7 %while.46 = (s32[]{:T(128)}, bf16[4,512,2048]{2,1,0:T(8,128)(2,1)}, s32[256]{0:T(256)S(1)}, s32[4]{0:T(128)S(1)}, s32[8]{0:T(128)S(1)}, /*index=5*/s32[2048]{0:T...) while((s32[]{:T(128)}, bf16[4,512,2048]{2,1,0:T(8,128)(2,1)}, ...), condition=%wide.region_26.27_spmd.clone, body=%wide.region_24.26_spmd.clone.sunk | while | flops 1095512832 | bytes 82248000 | solution.py:298
  441.7 7.8 fusion.226
  452.2 2.9 copy.170
  465.6 7.8 fusion.226
  476.1 2.9 copy.170
  489.6 7.8 fusion.226
  500.1 2.9 copy.170
  513.5 7.8 fusion.226
  524.0 2.9 copy.170
  528.8 6.6 convert_bitcast_fusion.1
  535.7 3.4 copy.163
  539.3 64.3 %while.49 = (s32[]{:T(128)}, f32[256,16,64]{0,2,1:T(8,128)}, s32[4]{0:T(128)S(1)}, bf16[2048,2048]{0,1:T(8,128)(2,1)}, s32[256]{0:T(256)S(1)}, /*index=5*/s32[8]...) while((s32[]{:T(128)}, f32[256,16,64]{0,2,1:T(8,128)}, ...), condition=%wide.region_23.24_spmd.clone, body=%wide.region_21.23_spmd.clone.sunk | while | flops 819213056 | bytes 27574568 | solution.py:61
  542.2 4.5 fusion.243
  547.2 7.9 fusion.244
  558.1 4.5 fusion.243
  563.0 8.3 fusion.244
  574.3 4.5 fusion.243
  579.3 8.1 fusion.244
  590.4 4.5 fusion.243
  595.4 8.2 fusion.244
  605.3 70.5 %reduce-scatter.15.cloned.1.call-done = bf16[256,2048]{1,0:T(8,128)(2,1)} async-done(((bf16[2048,2048]{1,0:T(8,128)(2,1)}), bf16[256,2048]{1,0:T(8,128)(2,1)}) %reduce-scatter.15.cloned.1.call-update) | async-done | bytes 1048592 | tf_op jit(solution)/shard_map/reduce_scatter | solution.py:301
  677.0 6.3 fusion.111
  687.5 7.7 fusion.117
  695.1 3.1 convert_reduce_fusion.4
  698.2 9.7 convolution_bitcast_fusion.1
  707.9 7.3 reduce-scatter.21.cloned.1.call-done
  717.9 5.5 all-to-all-start.1
  723.5 9.9 convolution_bitcast_fusion
  733.3 10.9 all-to-all-done.1
  749.6 102.5 %reduce-scatter.25.cloned.1.call-done = f32[32,7]{1,0:T(8,128)} async-done(((f32[1024,7]{1,0:T(8,128)}), f32[32,7]{1,0:T(8,128)}) %reduce-scatter.25.cloned.1.call-update) | async-done | bytes 912
  856.3 135.8 %reduce-scatter.19.cloned.1.call-done = f32[32,1024]{1,0:T(8,128)} async-done(((f32[1024,1024]{1,0:T(8,128)}), f32[32,1024]{1,0:T(8,128)}) %reduce-scatter.19.cloned.1.call-update) | async-done | bytes 131088 | tf_op jit(solution)/shard_map/reduce_scatter | solution.py:332
  992.1 157.9 %reduce-scatter.17.cloned.1.call-done = f32[32,3072]{1,0:T(8,128)} async-done(((f32[1024,3072]{1,0:T(8,128)}), f32[32,3072]{1,0:T(8,128)}) %reduce-scatter.17.cloned.1.call-update) | async-done | bytes 393232 | tf_op jit(solution)/shard_map/reduce_scatter | solution.py:331
  (296 shorter events, 123.6 us)
Async XLA Ops:
  7.2 245.0 %copy-start = (bf16[1024,1024]{1,0:T(8,128)(2,1)S(1)}, bf16[1024,1024]{1,0:T(8,128)(2,1)}, u32[]{:S(2)}) copy-start(bf16[1024,1024]{1,0:T(8,128)(2,1)} %param.29) | copy-start | bytes 6291460
  7.2 139.2 %all-gather.5.cloned.1.call-start = ((), (), s32[]{:S(2)}) async-start(), calls=%async_computation.10 | async-start | bytes 9437184 | tf_op jit(solution)/shard_map/all_gather | solution.py:163
  8.1 9.0 copy-start.17
  8.9 8.3 copy-start.15
  10.1 7.1 copy-start.19
  11.5 5.7 copy-start.21
  17.2 1.5 copy-start.31
  17.2 1.9 copy-start.26
  17.2 2.8 copy-start.28
  18.6 287.4 %all-gather.7.cloned.1.call-start = ((), (), s32[]{:S(2)}) async-start(), calls=%async_computation.11 | async-start | bytes 3932160 | tf_op jit(solution)/shard_map/all_gather | solution.py:194
  42.5 381.1 %copy-start.24 = (s32[256]{0:T(256)}, s32[256]{0:T(256)S(1)}, u32[]{:S(2)}) copy-start(s32[256]{0:T(256)S(1)} %multiply_add_fusion.1) | copy-start | bytes 3076
  210.2 41.9 %copy-start.7 = (bf16[1,256,1024]{2,1,0:T(8,128)(2,1)S(1)}, bf16[1,256,1024]{2,1,0:T(8,128)(2,1)}, u32[]{:S(2)}) copy-start(bf16[1,256,1024]{2,1,0:T(8,128)(2,1)} %param.23) | copy-start | bytes 1572868
  210.3 41.9 %copy-start.23 = (f32[1024]{0:T(1024)S(1)}, f32[1024]{0:T(1024)}, u32[]{:S(2)}) copy-start(f32[1024]{0:T(1024)} %param.30) | copy-start | bytes 12292
  252.1 2.4 copy-start.9
  253.0 1.0 copy-start.3
  253.0 53.0 %copy-start.30 = (f32[2,1024]{1,0:T(2,128)S(1)}, f32[2,1024]{1,0:T(2,128)}, u32[]{:S(2)}) copy-start(f32[2,1024]{1,0:T(2,128)} %param.32) | copy-start | bytes 24580
  278.4 57.8 %all-gather.9.cloned.1.call-start = ((), (), s32[]{:S(2)}) async-start(), calls=%async_computation.12 | async-start | bytes 3932160 | tf_op jit(solution)/shard_map/all_gather | solution.py:230
  304.2 91.1 %reduce-scatter.23.cloned.1.call-start = ((), (), s32[]{:S(2)}) async-start(), calls=%async_computation.17 | async-start | bytes 3932160
  336.2 13.0 %copy-start.29 = (bf16[2,1024,1024]{2,1,0:T(8,128)(2,1)S(1)}, bf16[2,1024,1024]{2,1,0:T(8,128)(2,1)}, u32[]{:S(2)}) copy-start(bf16[2,1024,1024]{2,1,0:T(8,128)(2,1)} %param.31) | copy-start | bytes 12582916
  349.2 4.2 copy-start.32
  357.2 68.6 %copy-start.14 = (bf16[1,256,1024]{2,1,0:T(8,128)(2,1)S(1)}, bf16[1,256,1024]{2,1,0:T(8,128)(2,1)}, u32[]{:S(2)}) copy-start(bf16[1,256,1024]{2,1,0:T(8,128)(2,1)} %param.24) | copy-start | bytes 1572868
  397.8 25.8 %all-to-all-start.3 = ((bf16[8,2,24,1024]{3,2,1,0:T(8,128)(2,1)}), bf16[8,2,24,1024]{3,2,1,0:T(8,128)(2,1)}, u32[]{:S(2)}, u32[]{:S(2)}) async-start(bf16[8,2,24,1024]{3,2,1,0:T(8,128)(2,1)} %bitcast.99), calls=%async_computation.3 | async-start | bytes 1572864 | tf_op jit(solution)/shard_map/all_to_all | solution.py:252
  403.3 272.5 %reduce-scatter.15.cloned.1.call-start = ((), (), s32[]{:S(2)}) async-start(), calls=%async_computation.13 | async-start | bytes 9437184 | tf_op jit(solution)/shard_map/reduce_scatter | solution.py:301
  427.6 1.0 copy-start.5
  437.0 3.2 copy-start.2
  460.9 3.2 copy-start.2
  484.9 3.2 copy-start.2
  508.8 3.2 copy-start.2
  528.5 6.8 copy-start.12
  528.5 186.7 %reduce-scatter.21.cloned.1.call-start = ((), (), s32[]{:S(2)}) async-start(), calls=%async_computation.16 | async-start | bytes 3932160
  539.1 313.0 %reduce-scatter.25.cloned.1.call-start = ((), (), s32[]{:S(2)}) async-start(), calls=%async_computation.18 | async-start | bytes 540672
  539.2 137.8 %copy-start.8 = (bf16[1,256,1024]{2,1,0:T(8,128)(2,1)S(1)}, bf16[1,256,1024]{2,1,0:T(8,128)(2,1)}, u32[]{:S(2)}) copy-start(bf16[1,256,1024]{2,1,0:T(8,128)(2,1)} %param.23) | copy-start | bytes 1572868
  539.2 137.8 %copy-start.16 = (f32[1,1024]{1,0:T(1,128)S(1)}, f32[1,1024]{1,0:T(1,128)}, u32[]{:S(2)}) copy-start(f32[1,1024]{1,0:T(1,128)} %copy-done.15) | copy-start | bytes 12292
  539.2 137.8 %copy-start.20 = (f32[256]{0:T(256)S(1)}, f32[256]{0:T(256)}, u32[]{:S(2)}) copy-start(f32[256]{0:T(256)} %copy-done.19) | copy-start | bytes 3076
  539.2 137.8 %copy-start.22 = (f32[256]{0:T(256)S(1)}, f32[256]{0:T(256)}, u32[]{:S(2)}) copy-start(f32[256]{0:T(256)} %copy-done.21) | copy-start | bytes 3076
  605.3 71.7 %copy-start.13 = (bf16[256,1024]{1,0:T(8,128)(2,1)}, bf16[256,1024]{1,0:T(8,128)(2,1)S(1)}, u32[]{:S(2)}) copy-start(bf16[256,1024]{1,0:T(8,128)(2,1)S(1)} %copy.115) | copy-start | bytes 1572868
  677.0 7.4 copy-start.6
  677.0 7.4 copy-start.10
  683.3 4.1 copy-start.11
  683.3 4.1 copy-start.18
  684.4 307.7 %reduce-scatter.19.cloned.1.call-start = ((), (), s32[]{:S(2)}) async-start(), calls=%async_computation.15 | async-start | bytes 4325376 | tf_op jit(solution)/shard_map/reduce_scatter | solution.py:332
  687.2 462.9 %reduce-scatter.17.cloned.1.call-start = ((), (), s32[]{:S(2)}) async-start(), calls=%async_computation.14 | async-start | bytes 12976128 | tf_op jit(solution)/shard_map/reduce_scatter | solution.py:331
  698.2 18.6 %copy-start.27 = (f32[2,1024]{1,0:T(2,128)S(1)}, f32[2,1024]{1,0:T(2,128)}, u32[]{:S(2)}) copy-start(f32[2,1024]{1,0:T(2,128)} %param.34) | copy-start | bytes 24580
  717.9 26.3 %all-to-all-start.1 = ((bf16[8,2,24,1024]{3,2,1,0:T(8,128)(2,1)}), bf16[8,2,24,1024]{3,2,1,0:T(8,128)(2,1)}, u32[]{:S(2)}, u32[]{:S(2)}) async-start(bf16[8,2,24,1024]{3,2,1,0:T(8,128)(2,1)} %copy.108), calls=%async_computation.1 | async-start | bytes 1572864 | tf_op jit(solution)/shard_map/all_to_all | solution.py:210
  723.5 20.8 %copy-start.4 = (f32[256,1024]{1,0:T(8,128)S(1)}, f32[256,1024]{1,0:T(8,128)}, u32[]{:S(2)}) copy-start(f32[256,1024]{1,0:T(8,128)} %copy-done.3) | copy-start | bytes 3145732
  723.5 20.8 %copy-start.25 = (s32[256]{0:T(256)S(1)}, s32[256]{0:T(256)}, u32[]{:S(2)}) copy-start(s32[256]{0:T(256)} %copy-done.24) | copy-start | bytes 3076
  723.5 426.6 %copy-start.1 = (bf16[1024,1024]{1,0:T(8,128)(2,1)S(1)}, bf16[1024,1024]{1,0:T(8,128)(2,1)}, u32[]{:S(2)}) copy-start(bf16[1024,1024]{1,0:T(8,128)(2,1)} %param.29) | copy-start | bytes 6291460
Sparse Core Ops, SparseCore 0:
  18.8 127.6 all-gather.4
  278.5 27.5 all-gather.6
  307.6 28.5 all-gather.8
  357.4 37.9 reduce-scatter.22
  528.6 147.1 reduce-scatter.14
  678.2 36.9 reduce-scatter.20
  717.5 134.5 reduce-scatter.24
  855.0 137.1 reduce-scatter.18
  998.8 151.2 reduce-scatter.16
where the time goes:
time: 1170 us; the launch traced here: 1160 us
  waiting for transfers between devices  658 us (56%)
  matrix products  228 us (19%)
  local copies, waits for them, and re-layouts  108 us (9%)
  blocking collectives  68.4 us (6%)
  other arithmetic  56.5 us (5%)
  between operations  14.9 us (1%)
  starting transfers between devices  12 us (1%)
    reduce_scatter x1, waiting for transfers between devices, local(): lax.psum_scatter(grad_w_qkv, ('seq', 'batch'), scatter_dimension=0, tiled...  158 us
    unnamed x12, waiting for transfers between devices  148 us
    reduce_scatter x1, waiting for transfers between devices, local(): lax.psum_scatter(grad_w_out, ('seq', 'batch'), scatter_dimension=0, tiled...  136 us
    all_gather x1, waiting for transfers between devices, local(): lax.all_gather(keys_vals, 'seq', axis=0, tiled=True)  104 us
    reduce_scatter x1, waiting for transfers between devices, local(): lax.psum_scatter(blocks.reshape(tok_rows * lax.axis_size('seq'), 2 * D).a...  70.5 us
    dot_general x8, matrix products, split_keys(): jnp.einsum('thd,khd->htk', query_h, key_h, preferred_element_type=jnp.flo...  37.1 us
    dot_general x4, matrix products, dquery_step(): jnp.einsum('htk,khd->thd', dscores, key_h, preferred_element_type=jnp.flo...  32.5 us
    dot_general x4, matrix products, key_grads(): jnp.einsum('hqk,qhd->khd', dscores, query_h, preferred_element_type=jnp.f...  31.2 us
  transfers between devices with their start and end apart: 11, of which 11 were waited for; matrix products, arithmetic and copies ran while one was open for 13% of the time, Pallas kernels for 0%

commit v1 on v0

--- a/solution.py
+++ b/solution.py
@@ -2,7 +2,10 @@
 
 import jax
 import jax.numpy as jnp
+import numpy as np
 from jax import lax
+from jax.experimental import pallas as pl
+from jax.experimental.pallas import tpu as pltpu
 from jax.sharding import PartitionSpec as P
 
 D = 1024
@@ -13,6 +16,46 @@
 
 EPS = 1e-05
 NEG = -1e30
+BIG = 1e30
+F32 = jnp.float32
+BF16 = jnp.bfloat16
+VMEM_LIMIT = 56 * 1024 * 1024
+
+
+def dot_nn(a, b):
+    return lax.dot_general(a, b, (((1,), (0,)), ((), ())), preferred_element_type=F32)
+
+
+def dot_nt(a, b):
+    return lax.dot_general(a, b, (((1,), (1,)), ((), ())), preferred_element_type=F32)
+
+
+def dot_tn(a, b):
+    return lax.dot_general(a, b, (((0,), (0,)), ((), ())), preferred_element_type=F32)
+
+
+def normed_rows(values):
+    centre = values - jnp.mean(values, axis=-1, keepdims=True)
+    spread = jnp.mean(centre * centre, axis=-1, keepdims=True)
+    inv_std = lax.rsqrt(spread + EPS)
+    return centre * inv_std, inv_std
+
+
+def whole(shape):
+    return pl.BlockSpec(shape, lambda *_: (0,) * len(shape))
+
+
+def params(**more):
+    return pltpu.CompilerParams(vmem_limit_bytes=VMEM_LIMIT, **more)
+
+
+def iota(shape, axis):
+    return lax.broadcasted_iota(jnp.int32, shape, axis)
+
+
+def running_sums(values):
+    upto = jnp.arange(values.shape[0])[:, None] >= jnp.arange(values.shape[0])[None, :]
+    return jnp.sum(jnp.where(upto, values[None, :], 0), axis=1)
 
 
 def layer_normalize(values, gain, shift):
@@ -115,7 +158,7 @@
     ).astype(jnp.bfloat16)
     query_h = queries.reshape(tok_rows, HEADS, HEAD_DIM)
     q_pos = lax.axis_index("seq") * tok_rows + jnp.arange(tok_rows, dtype=jnp.int32)
-    doc_ends = jnp.cumsum(doc_lengths[0])
+    doc_ends = running_sums(doc_lengths[0])
     q_doc = doc_of(q_pos, doc_ends)
     key_pad = pad_mask[0]
 
@@ -178,10 +221,8 @@
     )
     x_two = second_normalized.astype(jnp.bfloat16)
     token_ids = expert_ids[0, :, 0]
-    onehot = (token_ids[:, None] == jnp.arange(experts_all, dtype=jnp.int32)[None, :]).astype(
-        jnp.int32
-    )
-    ranks = jnp.sum((jnp.cumsum(onehot, axis=0) - onehot) * onehot, axis=1)
+    earlier = jnp.arange(tok_rows)[None, :] < jnp.arange(tok_rows)[:, None]
+    ranks = jnp.sum(((token_ids[:, None] == token_ids[None, :]) & earlier).astype(jnp.int32), axis=1)
     target = token_ids * capacity + ranks
     dispatch = (
         jnp.arange(experts_all * capacity, dtype=jnp.int32)[:, None] == target[None, :]
@@ -348,9 +389,938 @@
     )
 
 
+def qkv_kernel(n, T, cap, sc, *refs):
+    chunks = refs[: n - 1]
+    last_a, last_b = refs[n - 1 : n + 1]
+    wq, wk, wv, qvb, gain, bias, docs = refs[n + 1 : n + 8]
+    h_out, qkv_out, kaug_out, code_out, sel_out = refs[n + 8 : n + 13]
+    buf, w, sems = refs[n + 13 :]
+    split = last_a.shape[0]
+    copies = [
+        pltpu.make_async_copy(ref, buf.at[c], sems.at[c]) for c, ref in enumerate(chunks)
+    ]
+    copies.append(
+        pltpu.make_async_copy(last_a, buf.at[n - 1, pl.ds(0, split)], sems.at[n - 1])
+    )
+    copies.append(
+        pltpu.make_async_copy(
+            last_b, buf.at[n - 1, pl.ds(split, last_b.shape[0])], sems.at[n]
+        )
+    )
+    for copy in copies:
+        copy.start()
+    w[:, 0:128] = wq[...]
+    w[:, 128:256] = wk[...]
+    w[:, 256:384] = wv[...]
+    for copy in copies:
+        copy.wait()
+    me = sc[n]
+    g_row, b_row = gain[...], bias[...]
+
+    def one_chunk(c, carry):
+        src = sc[c]
+
+        def norm_part(r, carry2):
+            rows = pl.ds(pl.multiple_of(r * 64, 64), 64)
+            vhat, _ = normed_rows(buf[c, rows, :].astype(F32))
+            h_out[c, rows, :] = (vhat * g_row + b_row).astype(BF16)
+            return carry2
+
+        lax.fori_loop(0, T // 64, norm_part, 0)
+        rows = pl.ds(pl.multiple_of(src * T, T), T)
+        mixed = dot_nn(h_out[c], w[...])
+        q = (mixed[:, 0:128] + qvb[0:1, :]) * (HEAD_DIM**-0.5)
+        qkv_out[rows, 0:128] = q.astype(BF16)
+        qkv_out[rows, 128:256] = mixed[:, 128:256].astype(BF16)
+        qkv_out[rows, 256:384] = (mixed[:, 256:384] + qvb[1:2, :]).astype(BF16)
+        codes = buf[c, pl.ds(T, 16), :].astype(F32)
+        id_row = codes[0:1, 0:T]
+        pad_row = codes[0:1, T : 2 * T]
+        id_col = jnp.transpose(jnp.broadcast_to(id_row, (128, T)))
+        pad_col = jnp.transpose(jnp.broadcast_to(pad_row, (128, T)))
+        same = jnp.where(
+            (id_col[:, 0:1] == id_row) & (iota((T, T), 0) < iota((T, T), 1)), 1.0, 0.0
+        )
+        rank_row = jnp.sum(same, axis=0, keepdims=True)
+        rank_col = jnp.transpose(jnp.broadcast_to(rank_row, (128, T)))
+        lane = iota((T, 128), 1)
+        pos = (iota((T, 128), 0) + src * T).astype(F32)
+        doc = jnp.where((pos >= docs[0:1, :]) & (pos < docs[1:2, :]), 1.0, 0.0)
+        aug = jnp.where(lane < 8, doc, 0.0)
+        aug = jnp.where(lane == 8, 1.0 - pad_col, aug)
+        aug = jnp.where(lane == 16, id_col, aug)
+        aug = jnp.where(lane == 17, rank_col, aug)
+        kaug_out[rows, :] = aug.astype(BF16)
+        slot = (id_row * cap + rank_row).astype(jnp.int32)
+        half = lax.rem(src, 2) * cap
+        code_out[src] = (id_row * (2 * cap) + rank_row).astype(jnp.int32) + half
+        pick = jnp.where(
+            slot == iota((EXP_DEV * cap, T), 0) + me * (EXP_DEV * cap), 1.0, 0.0
+        ).astype(BF16)
+        chosen = dot_nn(pick, buf[c, pl.ds(0, T), :])
+        for e in range(EXP_DEV):
+            at = pl.multiple_of(e * n * cap + src * cap, 8)
+            sel_out[pl.ds(at, cap), :] = chosen[e * cap : (e + 1) * cap]
+        return carry
+
+    lax.fori_loop(0, n, one_chunk, 0)
+
+
+def qkv_call(n, T, cap, sc, chunks, w_qkv, qv_bias, gain, bias, docs):
+    rows = T + 16
+    anywhere = pl.BlockSpec(memory_space=pl.ANY)
+    in_specs = [anywhere] * (n + 1) + [
+        pl.BlockSpec((D, 128), lambda i, sc: (0, sc[n])),
+        pl.BlockSpec((D, 128), lambda i, sc: (0, n + sc[n])),
+        pl.BlockSpec((D, 128), lambda i, sc: (0, 2 * n + sc[n])),
+        pl.BlockSpec((2, 128), lambda i, sc: (0, sc[n])),
+        whole((1, D)),
+        whole((1, D)),
+        whole((2, 128)),
+    ]
+    shapes = [
+        ((n, T, D), BF16),
+        ((n * T, 384), BF16),
+        ((n * T, 128), BF16),
+        ((n, 1, T), jnp.int32),
+        ((EXP_DEV * n * cap, D), F32),
+    ]
+    return pl.pallas_call(
+        lambda *a: qkv_kernel(n, T, cap, *a),
+        grid_spec=pltpu.PrefetchScalarGridSpec(
+            num_scalar_prefetch=1,
+            grid=(1,),
+            in_specs=in_specs,
+            out_specs=[whole(s) for s, _ in shapes],
+            scratch_shapes=[
+                pltpu.VMEM((n, rows, D), BF16),
+                pltpu.VMEM((D, 384), BF16),
+                pltpu.SemaphoreType.DMA((n + 1,)),
+            ],
+        ),
+        out_shape=[jax.ShapeDtypeStruct(s, t) for s, t in shapes],
+        compiler_params=params(),
+        name="qkv",
+    )(sc, *chunks, w_qkv, w_qkv, w_qkv, qv_bias, gain, bias, docs)
+
+
+def head_split(n, T, qkv, kaug, qa, ka):
+    def part(r, carry):
+        rows = pl.ds(pl.multiple_of(r * T, T), T)
+        lane = iota((T, 128), 1)
+        q = qkv[rows, 0:128].astype(F32)
+        feature = kaug[rows, :].astype(F32)
+        extra = jnp.where(
+            lane < 8, (feature - 1.0) * BIG, jnp.where(lane == 8, -BIG, 0.0)
+        ).astype(BF16)
+        qa[0, rows, 0:128] = jnp.where(lane < HEAD_DIM, q, 0.0).astype(BF16)
+        qa[1, rows, 0:128] = jnp.where(lane >= HEAD_DIM, q, 0.0).astype(BF16)
+        qa[0, rows, 128:256] = extra
+        qa[1, rows, 128:256] = extra
+        ka[rows, 0:128] = qkv[rows, 128:256]
+        ka[rows, 128:256] = kaug[rows, :]
+        return carry
+
+    lax.fori_loop(0, n, part, 0)
+
+
+def diag_parts(T, kaug_rows):
+    lane = iota((T, 128), 1)
+    feature = kaug_rows.astype(F32)
+    unpadded = jnp.where(lane == 8, 0.0, feature).astype(BF16)
+    k_at, q_at = iota((T, T), 0), iota((T, T), 1)
+    padded = feature[:, 8:9] > 0.5
+    allowed = ((k_at < q_at) & jnp.logical_not(padded)) | (k_at == q_at)
+    return unpadded, allowed
+
+
+def attn_fwd_kernel(
+    n, T, cap, qkv, kaug, code, att_out, o_out, lse_out, qa, ka, vt, att, acc
+):
+    head_split(n, T, qkv, kaug, qa, ka)
+
+    def turn(r, carry):
+        rows = pl.ds(pl.multiple_of(r * T, T), T)
+        vt[r] = jnp.transpose(qkv[rows, 256:384].astype(F32)).astype(BF16)
+        return carry
+
+    lax.fori_loop(0, n, turn, 0)
+    halves = [slice(h * HEAD_DIM, (h + 1) * HEAD_DIM) for h in range(2)]
+
+    def query_block(i, carry):
+        rows = pl.ds(pl.multiple_of(i * T, T), T)
+        unpadded, allowed = diag_parts(T, kaug[rows, :])
+        kd = jnp.concatenate([qkv[rows, 128:256], unpadded], axis=1)
+        state = []
+        for h in range(2):
+            s = jnp.where(allowed, dot_nt(kd, qa[h, rows, :]), NEG)
+            top = jnp.max(s, axis=0, keepdims=True)
+            p = jnp.exp(s - top)
+            state += [top, jnp.sum(p, axis=0, keepdims=True)]
+            acc[halves[h], :] = dot_nn(vt[i, halves[h], :], p.astype(BF16))
+
+        def key_block(j, state):
+            cols = pl.ds(pl.multiple_of(j * T, T), T)
+            out = []
+            for h in range(2):
+                top, mass = state[2 * h : 2 * h + 2]
+                s = dot_nt(ka[cols, :], qa[h, rows, :])
+                new_top = jnp.maximum(top, jnp.max(s, axis=0, keepdims=True))
+                fade = jnp.exp(top - new_top)
+                p = jnp.exp(s - new_top)
+                out += [new_top, mass * fade + jnp.sum(p, axis=0, keepdims=True)]
+                acc[halves[h], :] = acc[halves[h], :] * fade + dot_nn(
+                    vt[j, halves[h], :], p.astype(BF16)
+                )
+            return tuple(out)
+
+        top0, mass0, top1, mass1 = lax.fori_loop(0, i, key_block, tuple(state))
+        lse_out[0, i] = top0 + jnp.log(mass0)
+        lse_out[1, i] = top1 + jnp.log(mass1)
+        o = jnp.transpose(
+            jnp.concatenate([acc[halves[0], :] / mass0, acc[halves[1], :] / mass1], axis=0)
+        )
+        o_out[rows, :] = o
+        att[rows, :] = o.astype(BF16)
+        return carry
+
+    lax.fori_loop(0, n, query_block, 0)
+    slots = n * EXP_DEV * 2 * cap
+
+    def pair(p, carry):
+        codes = jnp.concatenate([code[2 * p], code[2 * p + 1]], axis=1)
+        pick = jnp.where(codes == iota((slots, 2 * T), 0), 1.0, 0.0).astype(BF16)
+        chosen = dot_nn(pick, att[pl.ds(pl.multiple_of(p * 2 * T, 2 * T), 2 * T), :]).astype(
+            BF16
+        )
+        for k in range(n):
+            for e in range(EXP_DEV):
+                first = (k * EXP_DEV + e) * 2 * cap
+                at = pl.multiple_of(e * n * cap + p * 2 * cap, 16)
+                att_out[k, pl.ds(at, 2 * cap), :] = chosen[first : first + 2 * cap]
+        return carry
+
+    lax.fori_loop(0, n // 2, pair, 0)
+
+
+def attn_fwd_call(n, T, cap, qkv, kaug, code):
+    row = n * T
+    shapes = [
+        ((n, EXP_DEV * n * cap, 128), BF16),
+        ((row, 128), F32),
+        ((2, n, 1, T), F32),
+    ]
+    return pl.pallas_call(
+        lambda *a: attn_fwd_kernel(n, T, cap, *a),
+        out_shape=[jax.ShapeDtypeStruct(s, t) for s, t in shapes],
+        in_specs=[pl.BlockSpec(memory_space=pltpu.VMEM)] * 3,
+        out_specs=[pl.BlockSpec(memory_space=pltpu.VMEM)] * 3,
+        scratch_shapes=[
+            pltpu.VMEM((2, row, 256), BF16),
+            pltpu.VMEM((row, 256), BF16),
+            pltpu.VMEM((n, 128, T), BF16),
+            pltpu.VMEM((row, 128), BF16),
+            pltpu.VMEM((128, T), F32),
+        ],
+        compiler_params=params(),
+        name="attn_fwd",
+    )(qkv, kaug, code)
+
+
+def attn_bwd_kernel(
+    n, T, cap, qkv, kaug, lse, o_ref, datt, dm_out, ka_h, qa, v_h, kt, do, delta, dqt, dka, dva
+):
+    halves = [slice(h * HEAD_DIM, (h + 1) * HEAD_DIM) for h in range(2)]
+    slots = n * EXP_DEV * 2 * cap
+
+    def pair(p, carry):
+        rows = pl.ds(pl.multiple_of(p * 2 * T, 2 * T), 2 * T)
+        feature = kaug[rows, :].astype(F32)
+        at_row = iota((2 * T, 1), 0)
+        half = jnp.where(at_row >= T, float(cap), 0.0)
+        code = (feature[:, 16:17] * (2 * cap) + feature[:, 17:18] + half).astype(jnp.int32)
+        pick = jnp.where(code == iota((2 * T, slots), 1), 1.0, 0.0).astype(BF16)
+        parts = []
+        for k in range(n):
+            for e in range(EXP_DEV):
+                at = pl.multiple_of(e * n * cap + p * 2 * cap, 16)
+                parts.append(datt[k, pl.ds(at, 2 * cap), :])
+        got = dot_nn(pick, jnp.concatenate(parts, axis=0))
+        do[rows, :] = got.astype(BF16)
+        prod = jnp.transpose(got * o_ref[rows, :])
+        for h in range(2):
+            total = jnp.sum(prod[halves[h], :], axis=0, keepdims=True)
+            delta[h, 2 * p] = total[:, 0:T]
+            delta[h, 2 * p + 1] = total[:, T : 2 * T]
+        return carry
+
+    lax.fori_loop(0, n // 2, pair, 0)
+
+    def prepare(r, carry):
+        rows = pl.ds(pl.multiple_of(r * T, T), T)
+        lane = iota((T, 128), 1)
+        feature = kaug[rows, :].astype(F32)
+        extra = jnp.where(
+            lane < 8, (feature - 1.0) * BIG, jnp.where(lane == 8, -BIG, 0.0)
+        ).astype(BF16)
+        qa[rows, 0:128] = qkv[rows, 0:128]
+        qa[rows, 128:256] = extra
+        k = qkv[rows, 128:256].astype(F32)
+        v = qkv[rows, 256:384].astype(F32)
+        for h in range(2):
+            mine = (lane < HEAD_DIM) == (h == 0)
+            ka_h[h, rows, 0:128] = jnp.where(mine, k, 0.0).astype(BF16)
+            ka_h[h, rows, 128:256] = kaug[rows, :]
+            v_h[h, rows, :] = jnp.where(mine, v, 0.0).astype(BF16)
+        kt[r] = jnp.transpose(k).astype(BF16)
+        dqt[r] = jnp.zeros((128, T), F32)
+        return carry
+
+    lax.fori_loop(0, n, prepare, 0)
+
+    def tile(h, i, j, rows, key_rows, mask):
+        s = dot_nt(key_rows, qa[rows, :])
+        if mask is not None:
+            s = jnp.where(mask, s, NEG)
+        p = jnp.exp(s - lse[h, i])
+        dp = dot_nt(v_h[h, pl.ds(pl.multiple_of(j * T, T), T), :], do[rows, :])
+        ds = (p * (dp - delta[h, i])).astype(BF16)
+        dv = dot_nn(p.astype(BF16), do[rows, :])
+        dk = dot_nn(ds, qa[rows, 0:128])
+        dqt[i, halves[h], :] += dot_nn(kt[j, halves[h], :], ds)
+        return dk, dv
+
+    def key_block(j, carry):
+        cols = pl.ds(pl.multiple_of(j * T, T), T)
+        unpadded, allowed = diag_parts(T, kaug[cols, :])
+        for h in range(2):
+            kd = jnp.concatenate([ka_h[h, cols, 0:128], unpadded], axis=1)
+            dka[h], dva[h] = tile(h, j, j, cols, kd, allowed)
+
+        def query_block(i, carry2):
+            rows = pl.ds(pl.multiple_of(i * T, T), T)
+            for h in range(2):
+                dk, dv = tile(h, i, j, rows, ka_h[h, cols, :], None)
+                dka[h] += dk
+                dva[h] += dv
+            return carry2
+
+        lax.fori_loop(j + 1, n, query_block, 0)
+        lane = iota((T, 128), 1)
+        dm_out[j, :, 128:256] = jnp.where(lane < HEAD_DIM, dka[0], dka[1]).astype(BF16)
+        dm_out[j, :, 256:384] = jnp.where(lane < HEAD_DIM, dva[0], dva[1]).astype(BF16)
+        return carry
+
+    lax.fori_loop(0, n, key_block, 0)
+
+    def finish(i, carry):
+        dq = jnp.transpose(dqt[i]).astype(BF16).astype(F32)
+        dm_out[i, :, 0:128] = (dq * (HEAD_DIM**-0.5)).astype(BF16)
+        return carry
+
+    lax.fori_loop(0, n, finish, 0)
+
+
+def attn_bwd_call(n, T, cap, qkv, kaug, lse, o, datt):
+    row = n * T
+    return pl.pallas_call(
+        lambda *a: attn_bwd_kernel(n, T, cap, *a),
+        out_shape=jax.ShapeDtypeStruct((n, T, 384), BF16),
+        in_specs=[pl.BlockSpec(memory_space=pltpu.VMEM)] * 5,
+        out_specs=pl.BlockSpec(memory_space=pltpu.VMEM),
+        scratch_shapes=[
+            pltpu.VMEM((2, row, 256), BF16),
+            pltpu.VMEM((row, 256), BF16),
+            pltpu.VMEM((2, row, 128), BF16),
+            pltpu.VMEM((n, 128, T), BF16),
+            pltpu.VMEM((row, 128), BF16),
+            pltpu.VMEM((2, n, 1, T), F32),
+            pltpu.VMEM((n, 128, T), F32),
+            pltpu.VMEM((2, T, 128), F32),
+            pltpu.VMEM((2, T, 128), F32),
+        ],
+        compiler_params=params(),
+        name="attn_bwd",
+    )(qkv, kaug, lse, o, datt)
+
+
+def owner_fwd_kernel(n, att_in, w_out, sel, out_bias, gain, bias, x_two, x_one, att_b):
+    for k in range(n):
+        att_b[:, k * 128 : (k + 1) * 128] = att_in[k]
+    branch = dot_nn(att_b[...], w_out[...]) + out_bias[...]
+    x = sel[...] + branch
+    x_one[...] = x
+    vhat, _ = normed_rows(x)
+    x_two[...] = (vhat * gain[...] + bias[...]).astype(BF16)
+
+
+def owner_fwd_call(n, att_in, w_out, sel, out_bias, gain, bias):
+    slots = sel.shape[0]
+    block = 128
+    rows = pl.BlockSpec((block, D), lambda i: (i, 0))
+    return pl.pallas_call(
+        lambda *a: owner_fwd_kernel(n, *a),
+        grid=(slots // block,),
+        in_specs=[
+            pl.BlockSpec((n, block, 128), lambda i: (0, i, 0)),
+            whole((D, D)),
+            rows,
+            whole((1, D)),
+            whole((1, D)),
+            whole((1, D)),
+        ],
+        out_specs=[rows, rows, rows],
+        out_shape=[
+            jax.ShapeDtypeStruct((slots, D), BF16),
+            jax.ShapeDtypeStruct((slots, D), F32),
+            jax.ShapeDtypeStruct((slots, D), BF16),
+        ],
+        compiler_params=params(),
+        name="owner_fwd",
+    )(att_in, w_out, sel, out_bias, gain, bias)
+
+
+def owner_bwd_kernel(n, part_a, part_b, x_one, og, gain, w_out, datt, d_one_b, small):
+    u = (part_a[...].astype(F32) + part_b[...].astype(F32)).astype(BF16).astype(F32)
+    vhat, inv_std = normed_rows(x_one[...])
+    scaled = u * gain[...]
+    first = jnp.mean(scaled, axis=-1, keepdims=True)
+    second = jnp.mean(scaled * vhat, axis=-1, keepdims=True)
+    d_one = og[...].astype(F32) + inv_std * (scaled - first - vhat * second)
+    d_b = d_one.astype(BF16)
+    d_one_b[...] = d_b
+    back = dot_nt(d_b, w_out[...]).astype(BF16)
+    for k in range(n):
+        datt[k] = back[:, k * 128 : (k + 1) * 128]
+
+    @pl.when(pl.program_id(0) == 0)
+    def _():
+        small[...] = jnp.zeros_like(small)
+
+    small[0:1, :] += jnp.sum(u * vhat, axis=0, keepdims=True)
+    small[1:2, :] += jnp.sum(u, axis=0, keepdims=True)
+    small[2:3, :] += jnp.sum(d_one, axis=0, keepdims=True)
+
+
+def owner_bwd_call(n, part_a, part_b, x_one, og, gain, w_out):
+    slots = x_one.shape[0]
+    block = 128
+    rows = pl.BlockSpec((block, D), lambda i: (i, 0))
+    return pl.pallas_call(
+        lambda *a: owner_bwd_kernel(n, *a),
+        grid=(slots // block,),
+        in_specs=[rows, rows, rows, rows, whole((1, D)), whole((D, D))],
+        out_specs=[
+            pl.BlockSpec((n, block, 128), lambda i: (0, i, 0)),
+            rows,
+            whole((8, D)),
+        ],
+        out_shape=[
+            jax.ShapeDtypeStruct((n, slots, 128), BF16),
+            jax.ShapeDtypeStruct((slots, D), BF16),
+            jax.ShapeDtypeStruct((8, D), F32),
+        ],
+        compiler_params=params(),
+        name="owner_bwd",
+    )(part_a, part_b, x_one, og, gain, w_out)
+
+
+def expert_kernel(
+    nb, rows, steps, sc, *refs
+):
+    x_parts, g_parts = refs[:nb], refs[nb : 2 * nb]
+    w_in, b_in, w_out = refs[2 * nb : 2 * nb + 3]
+    hidden_out, dpre_out, keep, send, grad_b = refs[2 * nb + 3 : 2 * nb + 8]
+    xs, gs, total = refs[2 * nb + 8 :]
+    f = pl.program_id(1)
+
+    @pl.when(f == 0)
+    def _():
+        for k in range(nb):
+            xs[k * rows : (k + 1) * rows, :] = x_parts[k][...]
+            gs[k * rows : (k + 1) * rows, :] = g_parts[k][0]
+        total[...] = jnp.zeros_like(total)
+
+    pre = dot_nn(xs[...], w_in[0]) + b_in[0]
+    cdf = 0.5 * (1.0 + lax.erf(pre * (0.5**0.5)))
+    slope = cdf + pre * jnp.exp(-0.5 * pre * pre) * ((2.0 * math.pi) ** -0.5)
+    hidden_out[0] = (pre * cdf).astype(BF16)
+    dhidden = dot_nt(gs[...], w_out[0]).astype(BF16).astype(F32)
+    dpre = (dhidden * slope).astype(BF16)
+    dpre_out[0] = dpre
+    grad_b[0] = jnp.sum(dpre.astype(F32), axis=0, keepdims=True)
+    total[...] += dot_nt(dpre, w_in[0])
+
+    @pl.when(f == steps - 1)
+    def _():
+        for y in range(2):
+            keep[y] = total[2 * y * rows : (2 * y + 1) * rows, :].astype(BF16)
+            send[y] = total[(2 * y + 1) * rows : (2 * y + 2) * rows, :].astype(BF16)
+
+
+def expert_call(sc, x_parts, g_all, w_in, b_in, w_out):
+    nb = len(x_parts)
+    rows = x_parts[0].shape[0] // EXP_DEV
+    ff = w_in.shape[2]
+    width = min(256, ff)
+    steps = ff // width
+    g_specs = [
+        pl.BlockSpec((1, rows, D), lambda e, f, sc, k=k: (sc[0] ^ k, e, 0)) for k in range(nb)
+    ]
+    two = pl.BlockSpec((2, rows, D), lambda e, f, sc: (0, e, 0))
+    act = pl.BlockSpec((1, nb * rows, width), lambda e, f, sc: (e, 0, f))
+    return pl.pallas_call(
+        lambda *a: expert_kernel(nb, rows, steps, *a),
+        grid_spec=pltpu.PrefetchScalarGridSpec(
+            num_scalar_prefetch=1,
+            grid=(EXP_DEV, steps),
+            in_specs=[pl.BlockSpec((rows, D), lambda e, f, sc: (e, 0))] * nb
+            + g_specs
+            + [
+                pl.BlockSpec((1, D, width), lambda e, f, sc: (e, 0, f)),
+                pl.BlockSpec((1, 1, width), lambda e, f, sc: (e, 0, f)),
+                pl.BlockSpec((1, width, D), lambda e, f, sc: (e, f, 0)),
+            ],
+            out_specs=[act, act, two, two, pl.BlockSpec((1, 1, width), lambda e, f, sc: (e, 0, f))],
+            scratch_shapes=[
+                pltpu.VMEM((nb * rows, D), BF16),
+                pltpu.VMEM((nb * rows, D), BF16),
+                pltpu.VMEM((nb * rows, D), F32),
+            ],
+        ),
+        out_shape=[
+            jax.ShapeDtypeStruct((EXP_DEV, nb * rows, ff), BF16),
+            jax.ShapeDtypeStruct((EXP_DEV, nb * rows, ff), BF16),
+            jax.ShapeDtypeStruct((2, EXP_DEV * rows, D), BF16),
+            jax.ShapeDtypeStruct((2, EXP_DEV * rows, D), BF16),
+            jax.ShapeDtypeStruct((EXP_DEV, 1, ff), F32),
+        ],
+        compiler_params=params(),
+        name="expert_main",
+    )(sc, *x_parts, *([g_all] * nb), w_in, b_in[:, None, :], w_out)
+
+
+def expert_out_kernel(rows, hidden, w_out, keep, send):
+    total = dot_nn(hidden[0], w_out[0]).astype(BF16)
+    for y in range(2):
+        keep[y] = total[2 * y * rows : (2 * y + 1) * rows, :]
+        send[y] = total[(2 * y + 1) * rows : (2 * y + 2) * rows, :]
+
+
+def expert_out_call(hidden, w_out, nb):
+    rows = hidden.shape[1] // nb
+    ff = hidden.shape[2]
+    two = pl.BlockSpec((2, rows, D), lambda e: (0, e, 0))
+    return pl.pallas_call(
+        lambda *a: expert_out_kernel(rows, *a),
+        grid=(EXP_DEV,),
+        in_specs=[
+            pl.BlockSpec((1, nb * rows, ff), lambda e: (e, 0, 0)),
+            pl.BlockSpec((1, ff, D), lambda e: (e, 0, 0)),
+        ],
+        out_specs=[two, two],
+        out_shape=[jax.ShapeDtypeStruct((2, EXP_DEV * rows, D), BF16)] * 2,
+        compiler_params=params(),
+        name="expert_out",
+    )(hidden, w_out)
+
+
+def expert_grad_kernel(nb, rows, sc, *refs):
+    x_parts, g_parts = refs[:nb], refs[nb : 2 * nb]
+    hidden, dpre = refs[2 * nb : 2 * nb + 2]
+    grad_in, grad_out, grad_b = refs[2 * nb + 2 : 2 * nb + 5]
+    xs, gs = refs[2 * nb + 5 :]
+
+    @pl.when(pl.program_id(1) == 0)
+    def _():
+        sums = []
+        for k in range(nb):
+            xs[k * rows : (k + 1) * rows, :] = x_parts[k][...]
+            gs[k * rows : (k + 1) * rows, :] = g_parts[k][0]
+            sums.append(jnp.sum(g_parts[k][0].astype(F32), axis=0, keepdims=True))
+        grad_b[0] = (sums[0] + sums[1]) + (sums[2] + sums[3])
+
+    grad_in[0] = dot_tn(xs[...], dpre[0])
+    grad_out[0] = dot_tn(hidden[0], gs[...])
+
+
+def expert_grad_call(sc, x_parts, g_all, hidden, dpre):
+    nb = len(x_parts)
+    rows = x_parts[0].shape[0] // EXP_DEV
+    ff = hidden.shape[2]
+    width = min(256, ff)
+    g_specs = [
+        pl.BlockSpec((1, rows, D), lambda e, f, sc, k=k: (sc[0] ^ k, e, 0)) for k in range(nb)
+    ]
+    act = pl.BlockSpec((1, nb * rows, width), lambda e, f, sc: (e, 0, f))
+    return pl.pallas_call(
+        lambda *a: expert_grad_kernel(nb, rows, *a),
+        grid_spec=pltpu.PrefetchScalarGridSpec(
+            num_scalar_prefetch=1,
+            grid=(EXP_DEV, ff // width),
+            in_specs=[pl.BlockSpec((rows, D), lambda e, f, sc: (e, 0))] * nb
+            + g_specs
+            + [act, act],
+            out_specs=[
+                pl.BlockSpec((1, D, width), lambda e, f, sc: (e, 0, f)),
+                pl.BlockSpec((1, width, D), lambda e, f, sc: (e, f, 0)),
+                pl.BlockSpec((1, 1, D), lambda e, f, sc: (e, 0, 0)),
+            ],
+            scratch_shapes=[pltpu.VMEM((nb * rows, D), BF16)] * 2,
+        ),
+        out_shape=[
+            jax.ShapeDtypeStruct((EXP_DEV, D, ff), F32),
+            jax.ShapeDtypeStruct((EXP_DEV, ff, D), F32),
+            jax.ShapeDtypeStruct((EXP_DEV, 1, D), F32),
+        ],
+        compiler_params=params(),
+        name="expert_grads",
+    )(sc, *x_parts, *([g_all] * nb), hidden, dpre)
+
+
+def qkv_grad_kernel(n, nb, T, sc, h, dm, aux, keep, send, total):
+    me_b = sc[n + 1]
+
+    def add(c, carry):
+        total[...] += dot_tn(dm[sc[c]], h[c])
+        return carry
+
+    total[...] = jnp.zeros_like(total)
+    lax.fori_loop(0, n, add, 0)
+    col_sum = jnp.zeros((1, 384), F32)
+    for r in range(n):
+        col_sum = col_sum + jnp.sum(dm[r].astype(F32), axis=0, keepdims=True)
+    width = D // n
+    size = width // nb
+    top = iota((16, 384), 0)
+    for r in range(n):
+        part = jnp.transpose(total[:, r * width : (r + 1) * width])
+        for k in range(nb):
+            bb = me_b ^ k
+            rows = jnp.zeros((size, 384), F32)
+            for c in range(nb):
+                rows = jnp.where(bb == c, part[c * size : (c + 1) * size, :], rows)
+            extra = jnp.where(
+                top == 0, col_sum, jnp.where(top == 1, aux[r * nb + bb], 0.0)
+            )
+            to = keep if k % 2 == 0 else send
+            to[k // 2, r, 0:size, :] = rows.astype(BF16)
+            to[k // 2, r, size : size + 16, :] = extra.astype(BF16)
+
+
+def qkv_grad_call(n, nb, T, sc, h, dm, aux):
+    size = D // (n * nb)
+    shape = (2, n, size + 16, 384)
+    return pl.pallas_call(
+        lambda *a: qkv_grad_kernel(n, nb, T, *a),
+        grid_spec=pltpu.PrefetchScalarGridSpec(
+            num_scalar_prefetch=1,
+            grid=(1,),
+            in_specs=[whole((n, T, D)), whole((n, T, 384)), whole((n * nb, 1, 384))],
+            out_specs=[whole(shape), whole(shape)],
+            scratch_shapes=[pltpu.VMEM((384, D), F32)],
+        ),
+        out_shape=[jax.ShapeDtypeStruct(shape, BF16)] * 2,
+        compiler_params=params(),
+        name="qkv_grad",
+    )(sc, h, dm, aux)
+
+
+def scatter_rows(cap, slots, kaug, values):
+    feature = kaug.astype(F32)
+    code = (feature[:, 16:17] * cap + feature[:, 17:18]).astype(jnp.int32)
+    pick = jnp.where(code == iota((feature.shape[0], slots), 1), 1.0, 0.0).astype(BF16)
+    return dot_nn(pick, values)
+
+
+def input_grad_kernel(n, T, cap, sc, dm, w_qkv, hidden, d_ret, kaug, gain, out, full):
+    for k in range(n):
+        for part in range(3):
+            full[:, part * D + k * 128 : part * D + (k + 1) * 128] = dm[
+                k, :, part * 128 : (part + 1) * 128
+            ]
+    u = dot_nt(full[...], w_qkv[...])
+    vhat, inv_std = normed_rows(hidden[...].astype(F32))
+    scaled = u * gain[...]
+    first = jnp.mean(scaled, axis=-1, keepdims=True)
+    second = jnp.mean(scaled * vhat, axis=-1, keepdims=True)
+    d_one = scatter_rows(cap, d_ret.shape[0], kaug[...], d_ret[...])
+    out[...] = (d_one + inv_std * (scaled - first - vhat * second)).astype(BF16)
+
+
+def input_grad_call(n, T, cap, sc, dm, w_qkv, hidden, d_ret, kaug, gain):
+    slots = d_ret.shape[0]
+    return pl.pallas_call(
+        lambda *a: input_grad_kernel(n, T, cap, *a),
+        grid_spec=pltpu.PrefetchScalarGridSpec(
+            num_scalar_prefetch=1,
+            grid=(1,),
+            in_specs=[
+                whole((n, T, 384)),
+                whole((D, 3 * D)),
+                whole((T, D)),
+                whole((slots, D)),
+                pl.BlockSpec((T, 128), lambda i, sc: (sc[n], 0)),
+                whole((1, D)),
+            ],
+            out_specs=whole((T, D)),
+            scratch_shapes=[pltpu.VMEM((T, 3 * D), BF16)],
+        ),
+        out_shape=jax.ShapeDtypeStruct((T, D), BF16),
+        compiler_params=params(),
+        name="input_grad",
+    )(sc, dm, w_qkv, hidden, d_ret, kaug, gain)
+
+
+def output_kernel(cap, sc, ret, kaug, out):
+    out[...] = scatter_rows(cap, ret.shape[0], kaug[...], ret[...]).astype(BF16)
+
+
+def output_call(n, T, cap, sc, ret, kaug):
+    return pl.pallas_call(
+        lambda *a: output_kernel(cap, *a),
+        grid_spec=pltpu.PrefetchScalarGridSpec(
+            num_scalar_prefetch=1,
+            grid=(1,),
+            in_specs=[
+                whole(ret.shape),
+                pl.BlockSpec((T, 128), lambda i, sc: (sc[n], 0)),
+            ],
+            out_specs=whole((T, D)),
+        ),
+        out_shape=jax.ShapeDtypeStruct((T, D), BF16),
+        compiler_params=params(),
+        name="output_rows",
+    )(sc, ret, kaug)
+
+
+def final_kernel(n, nb, sc, got, w_rows, gb, gw, gains, biases, qvb, outb, s_rows, w_full):
+    size = D // (n * nb)
+    me, me_b = sc[n], sc[n + 1]
+    smalls = jnp.zeros((1, 384), F32)
+    s_rows[...] = jnp.zeros_like(s_rows)
+    for k in range(n):
+        tile = got[k].astype(F32)
+        for part in range(3):
+            cols = slice(part * D + k * 128, part * D + (k + 1) * 128)
+            w_full[:, cols] = tile[0:size, part * 128 : (part + 1) * 128]
+            s_rows[0:1, cols] = tile[size : size + 1, part * 128 : (part + 1) * 128]
+        smalls = smalls + tile[size + 1 : size + 2, :]
+    gw[...] = w_full[...]
+    weights = w_rows[...].astype(F32)
+    high = lax.Precision.HIGHEST
+    nt = (((1,), (1,)), ((), ()))
+    bias_one = lax.dot_general(s_rows[...], weights, nt, precision=high, preferred_element_type=F32)[0:1]
+    both = lax.dot_general(
+        jnp.ones((8, 3 * D), F32), weights * w_full[...], nt, precision=high, preferred_element_type=F32
+    )[0:1]
+    gains[0:1, :] = (both - gb[1:2, :] * bias_one) / gb[0:1, :]
+    gains[1:2, :] = smalls[:, 0:size]
+    biases[0:1, :] = bias_one
+    biases[1:2, :] = smalls[:, size : 2 * size]
+    outb[...] = smalls[:, 2 * size : 3 * size]
+    own = got[me, size : size + 16, :].astype(F32)[0:1]
+    for row, first in ((0, 0), (1, 256)):
+        value = jnp.zeros((1, size), F32)
+        for c in range(nb):
+            value = jnp.where(me_b == c, own[:, first + c * size : first + (c + 1) * size], value)
+        qvb[row : row + 1, :] = value
+
+
+def final_call(n, nb, sc, got, w_qkv, gb):
+    size = D // (n * nb)
+    shapes = [(size, 3 * D), (2, size), (2, size), (2, size), (1, size)]
+    return pl.pallas_call(
+        lambda *a: final_kernel(n, nb, *a),
+        grid_spec=pltpu.PrefetchScalarGridSpec(
+            num_scalar_prefetch=1,
+            grid=(1,),
+            in_specs=[
+                whole((n, size + 16, 384)),
+                pl.BlockSpec((size, 3 * D), lambda i, sc: (nb * sc[n] + sc[n + 1], 0)),
+                whole((2, size)),
+            ],
+            out_specs=[whole(s) for s in shapes],
+            scratch_shapes=[pltpu.VMEM((8, 3 * D), F32), pltpu.VMEM((size, 3 * D), F32)],
+        ),
+        out_shape=[jax.ShapeDtypeStruct(s, F32) for s in shapes],
+        compiler_params=params(),
+        name="final_rows",
+    )(sc, got, w_qkv, gb)
+
+
+def exchange(values, axis, bit):
+    size = lax.axis_size(axis)
+    return lax.ppermute(values, axis, [(i, i ^ bit) for i in range(size)])
+
+
+def gather_ring(payload, ring):
+    n = len(ring)
+    ahead = [(ring[i], ring[(i + 1) % n]) for i in range(n)]
+    back = [(ring[i], ring[i - 1]) for i in range(n)]
+    split = -(-payload.shape[0] // 32) * 16
+    chunks = [payload]
+    left = right = payload
+    for _ in range(n // 2 - 1):
+        left = lax.ppermute(left, "seq", ahead)
+        right = lax.ppermute(right, "seq", back)
+        chunks += [left, right]
+    return chunks + [
+        lax.ppermute(left[:split], "seq", ahead),
+        lax.ppermute(right[split:], "seq", back),
+    ]
+
+
+def reduce_batch(keep, send):
+    got = exchange(send, "batch", 1)
+    both = (keep.astype(F32) + got.astype(F32)).astype(BF16)
+    return both[0], exchange(both[1], "batch", 2)
+
+
+def local_by_heads(
+    hidden_in,
+    out_grad,
+    norm_gain_pair,
+    norm_bias_pair,
+    w_qkv,
+    qv_bias,
+    w_out,
+    out_bias,
+    w_in_exp,
+    b_in_exp,
+    w_out_exp,
+    b_out_exp,
+    expert_ids,
+    doc_lengths,
+    pad_mask,
+):
+    T = hidden_in.shape[1]
+    n, nb = lax.axis_size("seq"), lax.axis_size("batch")
+    experts = EXP_DEV * n
+    cap = max(2, 3 * T // (2 * experts))
+    s, b = lax.axis_index("seq"), lax.axis_index("batch")
+    ring = [*range(0, n, 2), *range(n - 1, 0, -2)]
+    place = [ring.index(i) for i in range(n)]
+    order = [0]
+    for step in range(1, n // 2):
+        order += [-step, step]
+    order += [n // 2]
+    table = np.array(
+        [[ring[(place[i] + o) % n] for o in order] + [i] for i in range(n)], np.int32
+    )
+    sc = jnp.concatenate(
+        [lax.dynamic_index_in_dim(jnp.asarray(table), s, 0, keepdims=False), b[None].astype(jnp.int32)]
+    )
+    sc_b = b[None].astype(jnp.int32)
+    hidden = hidden_in[0]
+    ids = expert_ids[0, :, 0]
+    codes = jnp.concatenate([ids, pad_mask[0], jnp.zeros((D - 2 * T,), jnp.int32)]).astype(BF16)
+    codes = jnp.where(jnp.arange(16)[:, None] == 0, codes[None, :], jnp.zeros((), BF16))
+    payload = jnp.concatenate([hidden, codes], axis=0)
+    chunks = gather_ring(payload, ring)
+
+    count = doc_lengths.shape[1]
+    at = jnp.arange(128)
+    ends = jnp.sum(
+        jnp.where(jnp.arange(count)[:, None] <= at[None, :], doc_lengths[0][:, None], 0), axis=0
+    )
+    starts = jnp.sum(
+        jnp.where(jnp.arange(count)[:, None] < at[None, :], doc_lengths[0][:, None], 0), axis=0
+    )
+    docs = jnp.stack([starts, ends]).astype(F32)
+    gain_rows = [norm_gain_pair[i : i + 1] for i in range(2)]
+    bias_rows = [norm_bias_pair[i : i + 1] for i in range(2)]
+
+    h_one, qkv, kaug, code, sel = qkv_call(
+        n, T, cap, sc, chunks, w_qkv, qv_bias, gain_rows[0], bias_rows[0], docs
+    )
+    same = (ids[:, None] == ids[None, :]) & (jnp.arange(T)[:, None] < jnp.arange(T)[None, :])
+    ranks = jnp.sum(same.astype(jnp.int32), axis=0)
+    slot = ids * cap + ranks
+    dispatch = (jnp.arange(experts * cap)[:, None] == slot[None, :]).astype(BF16)
+    sent_grads = dot_nn(dispatch, out_grad[0]).astype(BF16).reshape(n, EXP_DEV * cap, D)
+    grads = lax.all_to_all(sent_grads, "seq", split_axis=0, concat_axis=0, tiled=True)
+    grads = grads.reshape(n, EXP_DEV, cap, D).transpose(1, 0, 2, 3).reshape(experts * cap, D)
+    g_all = lax.all_gather(grads, "batch", axis=0, tiled=False)
+
+    att_out, o, lse = attn_fwd_call(n, T, cap, qkv, kaug, code)
+    att_in = lax.all_to_all(att_out, "seq", split_axis=0, concat_axis=0, tiled=True)
+    x_two, x_one, att_b = owner_fwd_call(
+        n, att_in, w_out, sel, out_bias[None], gain_rows[1], bias_rows[1]
+    )
+    x_core = exchange(x_two, "batch", 1)
+    x_y = exchange(x_two, "batch", 2)
+    x_far = exchange(x_y, "batch", 1)
+    x_parts = [x_two, x_core, x_y, x_far]
+    hidden_act, dpre, keep, send, grad_b_in = expert_call(
+        sc_b, x_parts, g_all, w_in_exp, b_in_exp, w_out_exp
+    )
+    part_a, part_b = reduce_batch(keep, send)
+    datt_out, d_one_b, small = owner_bwd_call(
+        n, part_a, part_b, x_one, grads, gain_rows[1], w_out
+    )
+    datt = lax.all_to_all(datt_out, "seq", split_axis=0, concat_axis=0, tiled=True)
+
+    keep_f, send_f = expert_out_call(hidden_act, w_out_exp, nb)
+    out_a, out_b = reduce_batch(keep_f, send_f)
+    expert_rows = (
+        (out_a.astype(F32) + out_b.astype(F32)).reshape(EXP_DEV, n * cap, D) + b_out_exp[:, None, :]
+    ).astype(BF16)
+    out_rows = (x_one.reshape(EXP_DEV, n * cap, D) + expert_rows.astype(F32)).astype(BF16)
+
+    def homeward(rows):
+        rows = rows.reshape(EXP_DEV, n, cap, D).transpose(1, 0, 2, 3)
+        rows = lax.all_to_all(rows, "seq", split_axis=0, concat_axis=0, tiled=True)
+        return rows.reshape(experts * cap, D)
+
+    d_ret = homeward(d_one_b)
+    out_ret = homeward(out_rows)
+    output = output_call(n, T, cap, sc, out_ret, kaug)
+
+    grad_w_in, grad_w_out_exp, grad_b_out = expert_grad_call(sc_b, x_parts, g_all, hidden_act, dpre)
+    size = D // (n * nb)
+    grad_w_out = dot_tn(att_b, d_one_b).astype(BF16).reshape(n, nb, size, D)
+    grad_w_out = lax.psum_scatter(grad_w_out, "batch", scatter_dimension=1, tiled=False)
+    grad_w_out = lax.psum_scatter(grad_w_out, "seq", scatter_dimension=0, tiled=False).astype(F32)
+
+    dm = attn_bwd_call(n, T, cap, qkv, kaug, lse, o, datt)
+    dm_own = lax.all_to_all(dm, "seq", split_axis=0, concat_axis=0, tiled=True)
+    aux = small[:3].reshape(3, n * nb, size).transpose(1, 0, 2).reshape(n * nb, 1, 3 * size)
+    aux = jnp.pad(aux, ((0, 0), (0, 0), (0, 384 - 3 * size)))
+    keep_w, send_w = qkv_grad_call(n, nb, T, sc, h_one, dm, aux)
+    w_a, w_b = reduce_batch(keep_w, send_w)
+    w_sum = (w_a.astype(F32) + w_b.astype(F32)).astype(BF16)
+    w_got = lax.all_to_all(w_sum, "seq", split_axis=0, concat_axis=0, tiled=True)
+    own = (s * nb + b) * size
+    gb = jnp.stack(
+        [
+            lax.dynamic_slice_in_dim(norm_gain_pair[0], own, size, 0),
+            lax.dynamic_slice_in_dim(norm_bias_pair[0], own, size, 0),
+        ]
+    )
+    gw_qkv, g_gains, g_biases, g_qvb, g_outb = final_call(n, nb, sc, w_got, w_qkv, gb)
+    input_grad = input_grad_call(n, T, cap, sc, dm_own, w_qkv, hidden, d_ret, kaug, gain_rows[0])
+    return (
+        output[None],
+        input_grad[None],
+        g_gains,
+        g_biases,
+        gw_qkv,
+        g_qvb,
+        grad_w_out,
+        g_outb[0],
+        grad_w_in,
+        grad_b_in[:, 0],
+        grad_w_out_exp,
+        grad_b_out[:, 0],
+    )
+
+
 def solution(mesh):
+    n, nb = mesh.shape["seq"], mesh.shape["batch"]
+    by_heads = HEADS * HEAD_DIM == 128 * n and nb == 4
     return jax.shard_map(
-        local,
+        local_by_heads if by_heads else local,
         mesh=mesh,
         in_specs=(
             P("batch", "seq", None),

time: 1170 us -> 450 us (0.38)
  waiting for transfers between devices: 658 us -> 159 us
  matrix products: 228 us -> 3.92 us
  Pallas kernels: 0 us -> 162 us
  local copies, waits for them, and re-layouts: 108 us -> 17.8 us
  other arithmetic: 56.5 us -> 11.3 us
  blocking collectives: 68.4 us -> 36.7 us
  starting transfers between devices: 12 us -> 43.6 us
    reduce_scatter x3 -> x2, waiting for transfers between devices: 364 us -> 28.6 us  [the longest x1 28.5 us: local_by_heads(): lax.psum_scatter(grad_w_out, 'seq', scatter_dimension=0, tiled=False)]
    dot_general x44 -> x2, matrix products: 228 us -> 3.92 us  [the longest x1 2.66 us: dot_tn(): lax.dot_general(a, b, (((0,), (0,)), ((), ())), preferred_element_type=F32)]
    pallas_call x0 -> x12, Pallas kernels: none -> 162 us  [the longest x1 33.9 us: attn_fwd_call(): pl.pallas_call(lambda *a: attn_fwd_kernel(n, T, cap, *a), out_shape=[jax....]
    unnamed x12 -> x3, waiting for transfers between devices: 148 us -> 0.69 us
    all_gather x3 -> x1, waiting for transfers between devices: 115 us -> 0.01 us  [local_by_heads(): g_all = lax.all_gather(grads, 'batch', axis=0, tiled=False)]
    ppermute x0 -> x17, waiting for transfers between devices: none -> 75.1 us  [the longest x9 42.7 us: exchange(): return lax.ppermute(values, axis, [(i, i ^ bit) for i in range(size)])]
    slice x23 -> x5, local copies, waits for them, and re-layouts: 35.3 us -> 1.25 us  [the longest x1 0.6 us: local_by_heads(): bias_rows = [norm_bias_pair[i:i + 1] for i in range(2)]]
    reduce_sum x29 -> x2, other arithmetic: 31.9 us -> 0.99 us  [the longest x1 0.91 us: local_by_heads(): ranks = jnp.sum(same.astype(jnp.int32), axis=0)]
  transfers between devices with their start and end apart: 11 -> 25, of which waited for: 11 -> 16; matrix products, arithmetic and copies ran while one was open for 13% -> 5% of each run, Pallas kernels for 0% -> 32%
where the time goes in v1:
time: 450 us; the launch traced here: 449 us
  Pallas kernels  162 us (36%)
  waiting for transfers between devices  159 us (35%)
  starting transfers between devices  43.6 us (10%)
  blocking collectives  36.7 us (8%)
  local copies, waits for them, and re-layouts  17.8 us (4%)
  between operations  14.2 us (3%)
  other arithmetic  11.3 us (3%)
    ppermute x9, waiting for transfers between devices, exchange(): return lax.ppermute(values, axis, [(i, i ^ bit) for i in range(size)])  42.7 us
    pallas_call x1, Pallas kernels, attn_fwd_call(): pl.pallas_call(lambda *a: attn_fwd_kernel(n, T, cap, *a), out_shape=[jax....  33.9 us
    pallas_call x1, Pallas kernels, attn_bwd_call(): pl.pallas_call(lambda *a: attn_bwd_kernel(n, T, cap, *a), out_shape=jax.S...  31.8 us
    reduce_scatter x1, waiting for transfers between devices, local_by_heads(): lax.psum_scatter(grad_w_out, 'seq', scatter_dimension=0, tiled=False)  28.5 us
    ppermute x3, waiting for transfers between devices, gather_ring(): right = lax.ppermute(right, 'seq', back)  24.6 us
    all_to_all x1, blocking collectives, local_by_heads(): lax.all_to_all(att_out, 'seq', split_axis=0, concat_axis=0, tiled=True)  22.6 us
    pallas_call x1, Pallas kernels, expert_call(): pl.pallas_call(lambda *a: expert_kernel(nb, rows, steps, *a), grid_spec=p...  19.9 us
    all_to_all x1, waiting for transfers between devices, local_by_heads(): lax.all_to_all(sent_grads, 'seq', split_axis=0, concat_axis=0, tiled=True)  19.2 us
  transfers between devices with their start and end apart: 25, of which 16 were waited for; matrix products, arithmetic and copies ran while one was open for 5% of the time, Pallas kernels for 32%

profile of v1, /device:TPU:0, one launch (start us, length us, event | category | flops | bytes accessed | tf_op | source)
XLA Modules:
  0.0 448.6 jit_solution(4710860705509690541)
XLA Ops:
  7.2 0.9 convert_reduce_fusion
  8.1 0.7 multiply_add_fusion
  8.8 1.3 convolution_convert_fusion.1
  10.1 7.2 %all-to-all-start.1 = ((bf16[8,48,1024]{2,1,0:T(8,128)(2,1)}), bf16[8,48,1024]{2,1,0:T(8,128)(2,1)S(1)}, u32[]{:S(2)}, u32[]{:S(2)}) async-start(bf16[8,48,1024]{2,1,0:T(8,128)(2,1)} %bitcast.10), calls=%async_computation.1 | async-start | bytes 1572864 | tf_op jit(solution)/shard_map/all_to_all | solution.py:1242
  17.6 2.0 collective-permute-start.1
  19.7 19.2 %all-to-all-done.1 = bf16[8,48,1024]{2,1,0:T(8,128)(2,1)S(1)} async-done(((bf16[8,48,1024]{2,1,0:T(8,128)(2,1)}), bf16[8,48,1024]{2,1,0:T(8,128)(2,1)S(1)}, u32[]{:S(2)}, u32[]{:S(2)}) %all-to-all-start.1) | async-done | bytes 786464 | tf_op jit(solution)/shard_map/all_to_all | solution.py:1242
  38.9 1.0 copy.56
  39.9 4.4 collective-permute-done.1.a_3_
  44.3 5.8 %collective-permute-start.2 = (bf16[272,1024]{1,0:T(8,128)(2,1)S(1)}, bf16[272,1024]{1,0:T(8,128)(2,1)S(1)}, u32[]{:S(2)}, u32[]{:S(2)}) collective-permute-start(bf16[272,1024]{1,0:T(8,128)(2,1)S(1)} %collective-permute-done.a_2_), channel_id=1, source_target_pairs={{0,8},{8,16},{16,24},{24,28},{28,20},{20,12},{12,4},{4,0},{1,9},{9... | collective-permute-start | bytes 1671176 | tf_op jit(solution)/shard_map/ppermute | solution.py:1165
  50.1 11.4 %collective-permute-done.3.a_5_ = bf16[272,1024]{1,0:T(8,128)(2,1)S(1)} collective-permute-done((bf16[272,1024]{1,0:T(8,128)(2,1)S(1)}, bf16[272,1024]{1,0:T(8,128)(2,1)S(1)}, u32[]{:S(2)}, u32[]{:S(2)}) %collective-permute-start.3) | collective-permute-done | bytes 557088 | tf_op jit(solution)/shard_map/ppermute | solution.py:1166
  62.1 1.5 collective-permute-start.4
  63.6 0.7 fusion.7
  65.5 8.7 %collective-permute-done.5.a_7_ = bf16[272,1024]{1,0:T(8,128)(2,1)S(1)} collective-permute-done((bf16[272,1024]{1,0:T(8,128)(2,1)S(1)}, bf16[272,1024]{1,0:T(8,128)(2,1)S(1)}, u32[]{:S(2)}, u32[]{:S(2)}) %collective-permute-start.5) | collective-permute-done | bytes 557088 | tf_op jit(solution)/shard_map/ppermute | solution.py:1166
  74.3 1.2 collective-permute-start.7
  75.5 1.1 collective-permute-done.4.a_6_
  76.7 0.7 pad_add_fusion.a_0_
  78.0 2.7 collective-permute-done.7.a_9_
  80.7 3.6 collective-permute-done.6.a_8_
  85.0 17.8 %qkv.1 = (bf16[8,256,1024]{2,1,0:T(8,128)(2,1)}, bf16[2048,384]{1,0:T(8,128)(2,1)}, bf16[2048,128]{1,0:T(8,128)(2,1)}, s32[8,1,256]{2,1,0:T(1,128)}, f32[384,1024]{1,0:T(8,128)}) custom-call(s32[10]{0:T(128)} %pad_add_fusion.a_0_, bf16[272,1024]{1,0:T(8,128)(2,1)} %copy-done.10, bf16[272,1024]{1,0:T(8,128)(2,1)} %copy-done.20, bf16[272,1024]{1,0:T(8,128)(2,1)} %copy-done.19, ...), custom_call_target="tpu_custom_call" | custom-call | tf_op jit(solution)/shard_map/qkv/pallas_call | solution.py:488
  102.8 33.9 %attn_fwd.1 = (bf16[8,384,128]{2,1,0:T(8,128)(2,1)}, f32[2048,128]{1,0:T(8,128)}, f32[2,8,1,256]{3,2,1,0:T(1,128)}) custom-call(bf16[2048,384]{1,0:T(8,128)(2,1)} %get-tuple-element.43.a_0_, bf16[2048,128]{1,0:T(8,128)(2,1)} %get-tuple-element.44.a_1_.a_2_.a_5_, s32[8,1,256]{2,1,0:T(1,128)} %get-tuple-element.45.a_2_), custom_call_target="tpu_custom_call" | custom-call | tf_op jit(solution)/shard_map/attn_fwd/pallas_call | solution.py:613
  136.8 22.6 %all_to_all.35.a_0_ = bf16[8,384,128]{2,1,0:T(8,128)(2,1)} all-to-all(bf16[8,384,128]{2,1,0:T(8,128)(2,1)} %get-tuple-element.46), channel_id=1, replica_groups=mesh['seq'=8,'batch'=4] {'seq'}, dimensions={0} | all-to-all | bytes 1572864 | tf_op jit(solution)/shard_map/all_to_all | solution.py:1247
  159.4 5.4 %owner_fwd.1 = (bf16[384,1024]{1,0:T(8,128)(2,1)}, f32[384,1024]{1,0:T(8,128)}, bf16[384,1024]{1,0:T(8,128)(2,1)}) custom-call(bf16[8,384,128]{2,1,0:T(8,128)(2,1)} %all_to_all.35.a_0_, bf16[1024,1024]{1,0:T(8,128)(2,1)} %a_5_.1, f32[384,1024]{1,0:T(8,128)} %get-tuple-element.47.a_2_, f32[1,1024]{1,0:T(1,128)} %bitcast.88, ...), custom_call_target="tpu_custom_call" | custom-call | tf_op jit(solution)/shard_map/owner_fwd/pallas_call | solution.py:761
  164.8 2.0 collective-permute-start.9
  166.8 15.8 %collective-permute-done.9.a_3_ = bf16[384,1024]{1,0:T(8,128)(2,1)S(1)} collective-permute-done((bf16[384,1024]{1,0:T(8,128)(2,1)}, bf16[384,1024]{1,0:T(8,128)(2,1)S(1)}, u32[]{:S(2)}, u32[]{:S(2)}) %collective-permute-start.9) | collective-permute-done | bytes 786464 | tf_op jit(solution)/shard_map/ppermute | solution.py:1154
  183.2 1.6 collective-permute-done.10.a_4_
  184.9 0.9 copy-done.6
  185.8 19.9 %expert_main.1 = (bf16[2,768,1024]{2,1,0:T(8,128)(2,1)}, bf16[2,768,1024]{2,1,0:T(8,128)(2,1)}, bf16[2,384,1024]{2,1,0:T(8,128)(2,1)}, bf16[2,384,1024]{2,1,0:T(8,128)(2,1)}, f32[2,1,1024]{2,1,0:T(1,128)}) custom-call(s32[1]{0:T(128)} %bitcast.1.a_0_, bf16[384,1024]{1,0:T(8,128)(2,1)} %get-tuple-element.49.a_1_, bf16[384,1024]{1,0:T(8,128)(2,1)} %copy-done.5, ...), custom_call_target="tpu_custom_call" | custom-call | tf_op jit(solution)/shard_map/expert_main/pallas_call | solution.py:872
  205.8 7.0 %expert_out.1 = (bf16[2,384,1024]{2,1,0:T(8,128)(2,1)}, bf16[2,384,1024]{2,1,0:T(8,128)(2,1)}) custom-call(bf16[2,768,1024]{2,1,0:T(8,128)(2,1)} %get-tuple-element.50.a_0_.a_9_, bf16[2,1024,1024]{2,1,0:T(8,128)(2,1)} %a_1_.3), custom_call_target="tpu_custom_call" | custom-call | tf_op jit(solution)/shard_map/expert_out/pallas_call | solution.py:914
  213.9 1.0 slice_bitcast_fusion
  214.9 1.7 collective-permute-start.14
  216.6 17.8 %collective-permute-done.14.a_1_ = bf16[384,1024]{1,0:T(8,128)(2,1)S(1)} collective-permute-done((bf16[384,1024]{1,0:T(8,128)(2,1)S(1)}, bf16[384,1024]{1,0:T(8,128)(2,1)S(1)}, u32[]{:S(2)}, u32[]{:S(2)}) %collective-permute-start.14) | collective-permute-done | bytes 786464 | tf_op jit(solution)/shard_map/ppermute | solution.py:1154
  234.5 0.9 copy-done.16
  235.4 7.1 %owner_bwd.1 = (bf16[8,384,128]{2,1,0:T(8,128)(2,1)}, bf16[384,1024]{1,0:T(8,128)(2,1)}, f32[8,1024]{1,0:T(8,128)}) custom-call(bf16[384,1024]{1,0:T(8,128)(2,1)} %get-tuple-element.77.a_0_, bf16[384,1024]{1,0:T(8,128)(2,1)} %copy-done.16, f32[384,1024]{1,0:T(8,128)} %get-tuple-element.48.a_2_, bf16[384,1024]{1,0:T(8,128)(2,1)} %bitcast.67, ...), custom_call_target="tpu_custom_call" | custom-call | tf_op jit(solution)/shard_map/owner_bwd/pallas_call | solution.py:809
  242.4 4.4 all-to-all-start.3
  246.8 1.1 copy-done.12
  248.0 2.6 add_convert_fusion.1
  250.6 0.9 slice_bitcast_fusion.2
  251.5 1.7 collective-permute-start.12
  253.3 1.0 copy.82
  254.2 12.3 %all-to-all-done.3.a_4_ = bf16[8,384,128]{2,1,0:T(8,128)(2,1)S(1)} async-done(((bf16[8,384,128]{2,1,0:T(8,128)(2,1)}), bf16[8,384,128]{2,1,0:T(8,128)(2,1)S(1)}, u32[]{:S(2)}, u32[]{:S(2)}) %all-to-all-start.3) | async-done | bytes 786464 | tf_op jit(solution)/shard_map/all_to_all | solution.py:1262
  266.5 0.9 copy-done.9
  267.4 3.5 all-to-all-start.5
  271.5 2.7 convolution_convert_fusion
  274.1 1.5 copy.63
  276.3 1.4 convert_add_fusion
  277.7 31.8 %attn_bwd.1.a_2_ = bf16[8,256,384]{2,1,0:T(8,128)(2,1)} custom-call(bf16[2048,384]{1,0:T(8,128)(2,1)} %get-tuple-element.43.a_0_, bf16[2048,128]{1,0:T(8,128)(2,1)} %get-tuple-element.44.a_1_.a_2_.a_5_, f32[2,8,1,256]{3,2,1,0:T(1,128)} %get-tuple-element.53.a_2_, f32[2048,128]{1,0:T(8,128)} %get-tuple-element.54.a_3_, bf16[8,384,128]{2,1,0:T(8,128)(2,1)} %copy-done.9), custom_call_target="tpu_custom_call" | custom-call | tf_op jit(solution)/shard_map/attn_bwd/pallas_call | solution.py:726
  309.5 8.4 %qkv_grad.1 = (bf16[2,8,48,384]{3,2,1,0:T(8,128)(2,1)}, bf16[2,8,48,384]{3,2,1,0:T(8,128)(2,1)}) custom-call(s32[10]{0:T(128)} %pad_add_fusion.a_0_, bf16[8,256,1024]{2,1,0:T(8,128)(2,1)} %get-tuple-element.59.a_1_, bf16[8,256,384]{2,1,0:T(8,128)(2,1)} %attn_bwd.1.a_2_, f32[32,1,384]{2,1,0:T(1,128)} %pad.4.a_3_), custom_call_target="tpu_custom_call" | custom-call | tf_op jit(solution)/shard_map/qkv_grad/pallas_call | solution.py:1014
  318.0 1.2 fusion.2
  319.2 5.8 %all-to-all-start.2 = ((bf16[8,2,24,1024]{3,2,1,0:T(8,128)(2,1)}), bf16[8,2,24,1024]{3,2,1,0:T(8,128)(2,1)S(1)}, u32[]{:S(2)}, u32[]{:S(2)}) async-start(bf16[8,2,24,1024]{3,2,1,0:T(8,128)(2,1)} %fusion.2), calls=%async_computation.2 | async-start | bytes 1572864 | tf_op jit(solution)/shard_map/all_to_all | solution.py:1273
  325.3 1.8 collective-permute-start.16
  327.1 7.4 %collective-permute-done.16 = bf16[8,48,384]{2,1,0:T(8,128)(2,1)S(1)} collective-permute-done((bf16[8,48,384]{2,1,0:T(8,128)(2,1)S(1)}, bf16[8,48,384]{2,1,0:T(8,128)(2,1)S(1)}, u32[]{:S(2)}, u32[]{:S(2)}) %collective-permute-start.16) | collective-permute-done | bytes 294944 | tf_op jit(solution)/shard_map/ppermute | solution.py:1154
  334.6 11.3 %all-to-all-done.2 = bf16[8,2,24,1024]{3,2,1,0:T(8,128)(2,1)S(1)} async-done(((bf16[8,2,24,1024]{3,2,1,0:T(8,128)(2,1)}), bf16[8,2,24,1024]{3,2,1,0:T(8,128)(2,1)S(1)}, u32[]{:S(2)}, u32[]{:S(2)}) %all-to-all-start.2) | async-done | bytes 786464 | tf_op jit(solution)/shard_map/all_to_all | solution.py:1273
  345.9 14.1 %all_to_all.36.a_1_ = bf16[8,48,384]{2,1,0:T(8,128)(2,1)} all-to-all(bf16[8,48,384]{2,1,0:T(8,128)(2,1)S(1)} %fusion.3), channel_id=1, replica_groups=mesh['seq'=8,'batch'=4] {'seq'}, dimensions={0} | all-to-all | bytes 589824 | tf_op jit(solution)/shard_map/all_to_all | solution.py:1293
  360.0 3.7 all-to-all-start.4
  365.1 0.7 constant_dynamic-slice_fusion
  366.9 17.0 %expert_grads.1 = (f32[2,1024,1024]{2,1,0:T(8,128)}, f32[2,1024,1024]{2,1,0:T(8,128)}, f32[2,1,1024]{2,1,0:T(1,128)}) custom-call(s32[1]{0:T(128)} %bitcast.1.a_0_, bf16[384,1024]{1,0:T(8,128)(2,1)} %get-tuple-element.49.a_1_, bf16[384,1024]{1,0:T(8,128)(2,1)} %copy-done.5, bf16[384,1024]{1,0:T(8,128)(2,1)} %copy-done.4, bf16[384,1024]{1,0:T(8,128)(2,1)} %copy-done.6, ...), custom_call_target="tpu_custom_call" | custom-call | tf_op jit(solution)/shard_map/expert_grads/pallas_call | solution.py:956
  384.0 1.3 copy.84
  385.3 3.2 output_rows.1
  388.5 3.0 final_rows.1
  391.5 11.9 %all-to-all-done.4.a_1_ = bf16[8,256,384]{2,1,0:T(8,128)(2,1)S(1)} async-done(((bf16[8,256,384]{2,1,0:T(8,128)(2,1)}), bf16[8,256,384]{2,1,0:T(8,128)(2,1)S(1)}, u32[]{:S(2)}, u32[]{:S(2)}) %all-to-all-start.4) | async-done | bytes 1572896 | tf_op jit(solution)/shard_map/all_to_all | solution.py:1287
  403.4 1.2 copy-done.2
  404.6 7.5 %input_grad.1 = bf16[256,1024]{1,0:T(8,128)(2,1)} custom-call(s32[10]{0:T(128)} %pad_add_fusion.a_0_, bf16[8,256,384]{2,1,0:T(8,128)(2,1)} %copy-done.2, bf16[1024,3072]{1,0:T(8,128)(2,1)} %a_2_.3, bf16[256,1024]{1,0:T(8,128)(2,1)} %bitcast.74, bf16[384,1024]{1,0:T(8,128)(2,1)} %bitcast.70, bf16[2048,128]{1,0:T(8,128)(2,1)} %get-tuple-element.44.a_1_.a_2_.a_5_, ...), custom_call_target="tpu_custom_call" | custom-call | tf_op jit(solution)/shard_map/input_grad/pallas_call | solution.py:1053
  412.1 28.5 %reduce-scatter.5.cloned.1.call-done = bf16[1,32,1024]{2,1,0:T(8,128)(2,1)} async-done(((bf16[8,32,1024]{2,1,0:T(8,128)(2,1)}), bf16[1,32,1024]{2,1,0:T(8,128)(2,1)}) %reduce-scatter.5.cloned.1.call-update) | async-done | bytes 65552 | tf_op jit(solution)/shard_map/reduce_scatter | solution.py:1284
  440.6 1.5 bitcast_convert_fusion
  (114 shorter events, 9.4 us)
Async XLA Ops:
  7.2 1.6 copy-start
  7.2 10.2 %copy-start.25 = (s32[1,256,1]{1,2,0:T(1,128)S(1)}, s32[1,256,1]{1,2,0:T(1,128)}, u32[]{:S(2)}) copy-start(s32[1,256,1]{1,2,0:T(1,128)} %param.28) | copy-start | bytes 3076
  7.2 10.2 %copy-start.32 = (s32[1,256]{1,0:T(1,128)S(1)}, s32[1,256]{1,0:T(1,128)}, u32[]{:S(2)}) copy-start(s32[1,256]{1,0:T(1,128)} %param.30) | copy-start | bytes 3076
  7.2 10.3 %copy-start.11 = (bf16[1,256,1024]{2,1,0:T(8,128)(2,1)S(1)}, bf16[1,256,1024]{2,1,0:T(8,128)(2,1)}, u32[]{:S(2)}) copy-start(bf16[1,256,1024]{2,1,0:T(8,128)(2,1)} %param.16) | copy-start | bytes 1572868
  10.1 28.8 %all-to-all-start.1 = ((bf16[8,48,1024]{2,1,0:T(8,128)(2,1)}), bf16[8,48,1024]{2,1,0:T(8,128)(2,1)S(1)}, u32[]{:S(2)}, u32[]{:S(2)}) async-start(bf16[8,48,1024]{2,1,0:T(8,128)(2,1)} %bitcast.10), calls=%async_computation.1 | async-start | bytes 1572864 | tf_op jit(solution)/shard_map/all_to_all | solution.py:1242
  17.3 167.5 %all-gather.2.cloned.1.call-start = ((), (), s32[]{:S(2)}) async-start(), calls=%async_computation.9 | async-start | bytes 3932160 | tf_op jit(solution)/shard_map/all_gather | solution.py:1244
  17.5 46.7 %copy-start.33 = (s32[1,8]{1,0:T(1,128)S(1)}, s32[1,8]{1,0:T(1,128)}, u32[]{:S(2)}) copy-start(s32[1,8]{1,0:T(1,128)} %param.29) | copy-start | bytes 100
  17.6 47.4 %copy-start.28 = (f32[2,1024]{1,0:T(2,128)S(1)}, f32[2,1024]{1,0:T(2,128)}, u32[]{:S(2)}) copy-start(f32[2,1024]{1,0:T(2,128)} %param.18) | copy-start | bytes 24580
  17.6 59.0 %copy-start.10 = (bf16[272,1024]{1,0:T(8,128)(2,1)}, bf16[272,1024]{1,0:T(8,128)(2,1)S(1)}, u32[]{:S(2)}) copy-start(bf16[272,1024]{1,0:T(8,128)(2,1)S(1)} %pad_maximum_fusion.a_1_) | copy-start | bytes 1671172
  17.6 26.7 %collective-permute-start.1 = (bf16[272,1024]{1,0:T(8,128)(2,1)S(1)}, bf16[272,1024]{1,0:T(8,128)(2,1)S(1)}, u32[]{:S(2)}, u32[]{:S(2)}) collective-permute-start(bf16[272,1024]{1,0:T(8,128)(2,1)S(1)} %pad_maximum_fusion.a_1_), channel_id=1, source_target_pairs={{0,4},{8,0},{16,8},{24,16},{28,24},{20,28},{12,20},{4,12},{1,5},{9... | collective-permute-start | bytes 1671176 | tf_op jit(solution)/shard_map/ppermute | solution.py:1166
  19.7 24.7 %collective-permute-start = (bf16[272,1024]{1,0:T(8,128)(2,1)S(1)}, bf16[272,1024]{1,0:T(8,128)(2,1)S(1)}, u32[]{:S(2)}, u32[]{:S(2)}) collective-permute-start(bf16[272,1024]{1,0:T(8,128)(2,1)S(1)} %pad_maximum_fusion.a_1_), channel_id=1, source_target_pairs={{0,8},{8,16},{16,24},{24,28},{28,20},{20,12},{12,4},{4,0},{1,9},{9... | collective-permute-start | bytes 1671176 | tf_op jit(solution)/shard_map/ppermute | solution.py:1165
  38.9 38.5 %copy-start.29 = (f32[2,1024]{1,0:T(2,128)S(1)}, f32[2,1024]{1,0:T(2,128)}, u32[]{:S(2)}) copy-start(f32[2,1024]{1,0:T(2,128)} %param.19) | copy-start | bytes 24580
  44.3 40.0 %copy-start.19 = (bf16[272,1024]{1,0:T(8,128)(2,1)}, bf16[272,1024]{1,0:T(8,128)(2,1)S(1)}, u32[]{:S(2)}) copy-start(bf16[272,1024]{1,0:T(8,128)(2,1)S(1)} %collective-permute-done.1.a_3_) | copy-start | bytes 1671172
  44.3 17.2 %collective-permute-start.3 = (bf16[272,1024]{1,0:T(8,128)(2,1)S(1)}, bf16[272,1024]{1,0:T(8,128)(2,1)S(1)}, u32[]{:S(2)}, u32[]{:S(2)}) collective-permute-start(bf16[272,1024]{1,0:T(8,128)(2,1)S(1)} %collective-permute-done.1.a_3_), channel_id=1, source_target_pairs={{0,4},{8,0},{16,8},{24,16},{28,24},{20,28},{12,20},{4,12},{1,5},{9... | collective-permute-start | bytes 1671176 | tf_op jit(solution)/shard_map/ppermute | solution.py:1166
  44.3 39.9 %copy-start.20 = (bf16[272,1024]{1,0:T(8,128)(2,1)}, bf16[272,1024]{1,0:T(8,128)(2,1)S(1)}, u32[]{:S(2)}) copy-start(bf16[272,1024]{1,0:T(8,128)(2,1)S(1)} %collective-permute-done.a_2_) | copy-start | bytes 1671172
  44.3 17.7 %collective-permute-start.2 = (bf16[272,1024]{1,0:T(8,128)(2,1)S(1)}, bf16[272,1024]{1,0:T(8,128)(2,1)S(1)}, u32[]{:S(2)}, u32[]{:S(2)}) collective-permute-start(bf16[272,1024]{1,0:T(8,128)(2,1)S(1)} %collective-permute-done.a_2_), channel_id=1, source_target_pairs={{0,8},{8,16},{16,24},{24,28},{28,20},{20,12},{12,4},{4,0},{1,9},{9... | collective-permute-start | bytes 1671176 | tf_op jit(solution)/shard_map/ppermute | solution.py:1165
  61.5 22.7 %copy-start.21 = (bf16[272,1024]{1,0:T(8,128)(2,1)}, bf16[272,1024]{1,0:T(8,128)(2,1)S(1)}, u32[]{:S(2)}) copy-start(bf16[272,1024]{1,0:T(8,128)(2,1)S(1)} %collective-permute-done.3.a_5_) | copy-start | bytes 1671172
  61.5 12.7 %collective-permute-start.5 = (bf16[272,1024]{1,0:T(8,128)(2,1)S(1)}, bf16[272,1024]{1,0:T(8,128)(2,1)S(1)}, u32[]{:S(2)}, u32[]{:S(2)}) collective-permute-start(bf16[272,1024]{1,0:T(8,128)(2,1)S(1)} %collective-permute-done.3.a_5_), channel_id=1, source_target_pairs={{0,4},{8,0},{16,8},{24,16},{28,24},{20,28},{12,20},{4,12},{1,5},{9... | collective-permute-start | bytes 1671176 | tf_op jit(solution)/shard_map/ppermute | solution.py:1166
  62.1 22.2 %copy-start.22 = (bf16[272,1024]{1,0:T(8,128)(2,1)}, bf16[272,1024]{1,0:T(8,128)(2,1)S(1)}, u32[]{:S(2)}) copy-start(bf16[272,1024]{1,0:T(8,128)(2,1)S(1)} %collective-permute-done.2.a_4_) | copy-start | bytes 1671172
  62.1 14.5 %collective-permute-start.4 = (bf16[272,1024]{1,0:T(8,128)(2,1)S(1)}, bf16[272,1024]{1,0:T(8,128)(2,1)S(1)}, u32[]{:S(2)}, u32[]{:S(2)}) collective-permute-start(bf16[272,1024]{1,0:T(8,128)(2,1)S(1)} %collective-permute-done.2.a_4_), channel_id=1, source_target_pairs={{0,8},{8,16},{16,24},{24,28},{28,20},{20,12},{12,4},{4,0},{1,9},{9... | collective-permute-start | bytes 1671176 | tf_op jit(solution)/shard_map/ppermute | solution.py:1165
  74.3 10.0 %copy-start.15 = (bf16[272,1024]{1,0:T(8,128)(2,1)}, bf16[272,1024]{1,0:T(8,128)(2,1)S(1)}, u32[]{:S(2)}) copy-start(bf16[272,1024]{1,0:T(8,128)(2,1)S(1)} %collective-permute-done.5.a_7_) | copy-start | bytes 1671172
  74.3 6.4 %collective-permute-start.7 = (bf16[128,1024]{1,0:T(8,128)(2,1)S(1)}, bf16[128,1024]{1,0:T(8,128)(2,1)S(1)}, u32[]{:S(2)}, u32[]{:S(2)}) collective-permute-start(bf16[128,1024]{1,0:T(8,128)(2,1)S(1)} %slice.55), channel_id=1, source_target_pairs={{0,4},{8,0},{16,8},{24,16},{28,24},{20,28},{12,20},{4,12},{1,5},{9... | collective-permute-start | bytes 786440 | tf_op jit(solution)/shard_map/ppermute | solution.py:1170
  76.6 7.7 %copy-start.14 = (bf16[272,1024]{1,0:T(8,128)(2,1)}, bf16[272,1024]{1,0:T(8,128)(2,1)S(1)}, u32[]{:S(2)}) copy-start(bf16[272,1024]{1,0:T(8,128)(2,1)S(1)} %collective-permute-done.4.a_6_) | copy-start | bytes 1671172
  76.7 7.6 %collective-permute-start.6 = (bf16[144,1024]{1,0:T(8,128)(2,1)S(1)}, bf16[144,1024]{1,0:T(8,128)(2,1)S(1)}, u32[]{:S(2)}, u32[]{:S(2)}) collective-permute-start(bf16[144,1024]{1,0:T(8,128)(2,1)S(1)} %slice.54), channel_id=1, source_target_pairs={{0,8},{8,16},{16,24},{24,28},{28,20},{20,12},{12,4},{4,0},{1,9},{9... | collective-permute-start | bytes 884744 | tf_op jit(solution)/shard_map/ppermute | solution.py:1169
  80.7 3.6 copy-start.24
  84.3 0.7 copy-start.23
  159.4 23.2 %copy-start.30 = (f32[2,1024]{1,0:T(2,128)S(1)}, f32[2,1024]{1,0:T(2,128)}, u32[]{:S(2)}) copy-start(f32[2,1024]{1,0:T(2,128)} %param.25) | copy-start | bytes 24580
  164.8 17.8 %collective-permute-start.9 = (bf16[384,1024]{1,0:T(8,128)(2,1)}, bf16[384,1024]{1,0:T(8,128)(2,1)S(1)}, u32[]{:S(2)}, u32[]{:S(2)}) collective-permute-start(bf16[384,1024]{1,0:T(8,128)(2,1)} %get-tuple-element.49.a_1_), channel_id=1, source_target_pairs={{0,2},{1,3},{2,0},{3,1},{4,6},{5,7},{6,4},{7,5},{8,10},{9,11},{10,... | collective-permute-start | bytes 2359304 | tf_op jit(solution)/shard_map/ppermute | solution.py:1154
  166.8 16.5 %collective-permute-start.8 = (bf16[384,1024]{1,0:T(8,128)(2,1)}, bf16[384,1024]{1,0:T(8,128)(2,1)S(1)}, u32[]{:S(2)}, u32[]{:S(2)}) collective-permute-start(bf16[384,1024]{1,0:T(8,128)(2,1)} %get-tuple-element.49.a_1_), channel_id=1, source_target_pairs={{0,1},{1,0},{2,3},{3,2},{4,5},{5,4},{6,7},{7,6},{8,9},{9,8},{10,11... | collective-permute-start | bytes 2359304 | tf_op jit(solution)/shard_map/ppermute | solution.py:1154
  182.6 2.3 copy-start.4
  182.6 2.3 collective-permute-start.10
  183.2 1.6 copy-start.5
  184.8 0.9 copy-start.6
  205.6 7.6 %collective-permute-start.13 = (bf16[2,384,1024]{2,1,0:T(8,128)(2,1)}, bf16[2,384,1024]{2,1,0:T(8,128)(2,1)S(1)}, u32[]{:S(2)}, u32[]{:S(2)}) collective-permute-start(bf16[2,384,1024]{2,1,0:T(8,128)(2,1)} %get-tuple-element.56), channel_id=1, source_target_pairs={{0,1},{1,0},{2,3},{3,2},{4,5},{5,4},{6,7},{7,6},{8,9},{9,8},{10,11... | collective-permute-start | bytes 4718600 | tf_op jit(solution)/shard_map/ppermute | solution.py:1154
  205.8 7.4 %copy-start.13 = (bf16[2,384,1024]{2,1,0:T(8,128)(2,1)S(1)}, bf16[2,384,1024]{2,1,0:T(8,128)(2,1)}, u32[]{:S(2)}) copy-start(bf16[2,384,1024]{2,1,0:T(8,128)(2,1)} %get-tuple-element.55) | copy-start | bytes 4718596
  212.8 34.0 %collective-permute-start.11 = (bf16[2,384,1024]{2,1,0:T(8,128)(2,1)}, bf16[2,384,1024]{2,1,0:T(8,128)(2,1)S(1)}, u32[]{:S(2)}, u32[]{:S(2)}) collective-permute-start(bf16[2,384,1024]{2,1,0:T(8,128)(2,1)} %get-tuple-element.52), channel_id=1, source_target_pairs={{0,1},{1,0},{2,3},{3,2},{4,5},{5,4},{6,7},{7,6},{8,9},{9,8},{10,11... | collective-permute-start | bytes 4718600 | tf_op jit(solution)/shard_map/ppermute | solution.py:1154
  214.9 19.6 %collective-permute-start.14 = (bf16[384,1024]{1,0:T(8,128)(2,1)S(1)}, bf16[384,1024]{1,0:T(8,128)(2,1)S(1)}, u32[]{:S(2)}, u32[]{:S(2)}) collective-permute-start(bf16[384,1024]{1,0:T(8,128)(2,1)S(1)} %get-tuple-element.76), channel_id=1, source_target_pairs={{0,2},{1,3},{2,0},{3,1},{4,6},{5,7},{6,4},{7,5},{8,10},{9,11},{10,... | collective-permute-start | bytes 2359304 | tf_op jit(solution)/shard_map/ppermute | solution.py:1154
  234.5 0.9 copy-start.16
  242.4 24.1 %all-to-all-start.3 = ((bf16[8,384,128]{2,1,0:T(8,128)(2,1)}), bf16[8,384,128]{2,1,0:T(8,128)(2,1)S(1)}, u32[]{:S(2)}, u32[]{:S(2)}) async-start(bf16[8,384,128]{2,1,0:T(8,128)(2,1)} %get-tuple-element.57), calls=%async_computation.3 | async-start | bytes 1572864 | tf_op jit(solution)/shard_map/all_to_all | solution.py:1262
  246.8 1.1 copy-start.12
  250.5 2.7 copy-start.17
  251.5 24.8 %collective-permute-start.12 = (bf16[384,1024]{1,0:T(8,128)(2,1)}, bf16[384,1024]{1,0:T(8,128)(2,1)}, u32[]{:S(2)}, u32[]{:S(2)}) collective-permute-start(bf16[384,1024]{1,0:T(8,128)(2,1)} %slice_bitcast_fusion.2), channel_id=1, source_target_pairs={{0,2},{1,3},{2,0},{3,1},{4,6},{5,7},{6,4},{7,5},{8,10},{9,11},{10,... | collective-permute-start | bytes 2359304 | tf_op jit(solution)/shard_map/ppermute | solution.py:1154
  253.2 18.0 %copy-start.27 = (f32[8,1024]{1,0:T(8,128)S(1)}, f32[8,1024]{1,0:T(8,128)}, u32[]{:S(2)}) copy-start(f32[8,1024]{1,0:T(8,128)} %get-tuple-element.60) | copy-start | bytes 98308
  266.5 0.9 copy-start.9
  267.4 51.8 %all-to-all-start.5 = ((bf16[8,2,24,1024]{3,2,1,0:T(8,128)(2,1)}), bf16[8,2,24,1024]{3,2,1,0:T(8,128)(2,1)S(1)}, u32[]{:S(2)}, u32[]{:S(2)}) async-start(bf16[8,2,24,1024]{3,2,1,0:T(8,128)(2,1)} %bitcast.72), calls=%async_computation.5 | async-start | bytes 1572864 | tf_op jit(solution)/shard_map/all_to_all | solution.py:1273
  271.0 92.8 %reduce-scatter.3.cloned.1.call-start = ((), (), s32[]{:S(2)}) async-start(), calls=%async_computation.10 | async-start | bytes 2621440 | tf_op jit(solution)/shard_map/reduce_scatter | solution.py:1283
  309.5 8.5 %copy-start.3 = (f32[384,1024]{1,0:T(8,128)S(1)}, f32[384,1024]{1,0:T(8,128)}, u32[]{:S(2)}) copy-start(f32[384,1024]{1,0:T(8,128)} %get-tuple-element.48.a_2_) | copy-start | bytes 4718596
  309.5 8.5 %copy-start.26 = (f32[2,1024]{1,0:T(2,128)S(1)}, f32[2,1024]{1,0:T(2,128)}, u32[]{:S(2)}) copy-start(f32[2,1024]{1,0:T(2,128)} %param.27) | copy-start | bytes 24580
  318.0 7.1 %collective-permute-start.15 = (bf16[2,8,48,384]{3,2,1,0:T(8,128)(2,1)}, bf16[2,8,48,384]{3,2,1,0:T(8,128)(2,1)S(1)}, u32[]{:S(2)}, u32[]{:S(2)}) collective-permute-start(bf16[2,8,48,384]{3,2,1,0:T(8,128)(2,1)} %get-tuple-element.62), channel_id=1, source_target_pairs={{0,1},{1,0},{2,3},{3,2},{4,5},{5,4},{6,7},{7,6},{8,9},{9,8},{10,11... | collective-permute-start | bytes 1769480 | tf_op jit(solution)/shard_map/ppermute | solution.py:1154
  319.2 5.9 %copy-start.18 = (bf16[2,8,48,384]{3,2,1,0:T(8,128)(2,1)S(1)}, bf16[2,8,48,384]{3,2,1,0:T(8,128)(2,1)}, u32[]{:S(2)}) copy-start(bf16[2,8,48,384]{3,2,1,0:T(8,128)(2,1)} %get-tuple-element.61) | copy-start | bytes 1769476
  319.2 6.0 %copy-start.7 = (bf16[8,2,24,1024]{3,2,1,0:T(8,128)(2,1)}, bf16[8,2,24,1024]{3,2,1,0:T(8,128)(2,1)S(1)}, u32[]{:S(2)}) copy-start(bf16[8,2,24,1024]{3,2,1,0:T(8,128)(2,1)S(1)} %all-to-all-done.5) | copy-start | bytes 2359300
  319.2 26.7 %all-to-all-start.2 = ((bf16[8,2,24,1024]{3,2,1,0:T(8,128)(2,1)}), bf16[8,2,24,1024]{3,2,1,0:T(8,128)(2,1)S(1)}, u32[]{:S(2)}, u32[]{:S(2)}) async-start(bf16[8,2,24,1024]{3,2,1,0:T(8,128)(2,1)} %fusion.2), calls=%async_computation.2 | async-start | bytes 1572864 | tf_op jit(solution)/shard_map/all_to_all | solution.py:1273
  325.3 9.2 %collective-permute-start.16 = (bf16[8,48,384]{2,1,0:T(8,128)(2,1)S(1)}, bf16[8,48,384]{2,1,0:T(8,128)(2,1)S(1)}, u32[]{:S(2)}, u32[]{:S(2)}) collective-permute-start(bf16[8,48,384]{2,1,0:T(8,128)(2,1)S(1)} %slice_bitcast_fusion.4), channel_id=1, source_target_pairs={{0,2},{1,3},{2,0},{3,1},{4,6},{5,7},{6,4},{7,5},{8,10},{9,11},{10,... | collective-permute-start | bytes 884744 | tf_op jit(solution)/shard_map/ppermute | solution.py:1154
  345.9 14.1 %copy-start.8 = (bf16[8,2,24,1024]{3,2,1,0:T(8,128)(2,1)}, bf16[8,2,24,1024]{3,2,1,0:T(8,128)(2,1)S(1)}, u32[]{:S(2)}) copy-start(bf16[8,2,24,1024]{3,2,1,0:T(8,128)(2,1)S(1)} %all-to-all-done.2) | copy-start | bytes 2359300
  360.0 6.4 %copy-start.31 = (f32[2,1,1024]{2,1,0:T(1,128)S(1)}, f32[2,1,1024]{2,1,0:T(1,128)}, u32[]{:S(2)}) copy-start(f32[2,1,1024]{2,1,0:T(1,128)} %get-tuple-element.71) | copy-start | bytes 24580
  360.0 43.4 %all-to-all-start.4 = ((bf16[8,256,384]{2,1,0:T(8,128)(2,1)}), bf16[8,256,384]{2,1,0:T(8,128)(2,1)S(1)}, u32[]{:S(2)}, u32[]{:S(2)}) async-start(bf16[8,256,384]{2,1,0:T(8,128)(2,1)} %attn_bwd.1.a_2_), calls=%async_computation.4 | async-start | bytes 3145728 | tf_op jit(solution)/shard_map/all_to_all | solution.py:1287
  363.7 76.9 %reduce-scatter.5.cloned.1.call-start = ((), (), s32[]{:S(2)}) async-start(), calls=%async_computation.11 | async-start | bytes 589824 | tf_op jit(solution)/shard_map/reduce_scatter | solution.py:1284
  403.4 1.2 copy-start.2
  404.6 37.5 %copy-start.1 = (bf16[1,256,1024]{2,1,0:T(8,128)(2,1)S(1)}, bf16[1,256,1024]{2,1,0:T(8,128)(2,1)}, u32[]{:S(2)}) copy-start(bf16[1,256,1024]{2,1,0:T(8,128)(2,1)} %param.17) | copy-start | bytes 1572868
Sparse Core Ops, SparseCore 0:
  40.0 26.2 all-gather.1
  275.8 32.8 reduce-scatter.2
  368.2 72.3 reduce-scatter.4
